TPU v7x, 128 devices: a whole 4x4x4 slice. The times are simulated.
128 devices in a mesh: tok: 32 (over y, x_lo, z), rep: 4 (over x_hi, core).
Axes of the slice: x: 4 (x_hi: 2, x_lo: 2; x = x_hi * 2 + x_lo), y: 4, z: 4, core: 2. Of those that a mesh axis runs over, the one named last changes fastest.
Arguments:
- tokens: bfloat16 [65536, 768], P(('rep', 'tok')), parts along dimension 0, may hold values from -6 to 6
- attn_gain: bfloat16 [768], replicated, may hold values from 0.25 to 1.75
- qkv_weight: bfloat16 [768, 2304], replicated, may hold values from -0.21875 to 0.21875
- head_temp: float32 [12], replicated, may hold values from 2 to 600, as said below
- out_weight: bfloat16 [768, 768], replicated, may hold values from -0.21875 to 0.21875
- kv_weight: bfloat16 [768, 1536], replicated, may hold values from -0.21875 to 0.21875
- rate_weight: float32 [768, 2], replicated, may hold values from -0.21875 to 0.21875
- fast_weights: bfloat16 [768, 2304], replicated, may hold values from -0.3125 to 0.3125
- target: bfloat16 [32768, 768], P(('rep', 'tok')), parts along dimension 0, may hold values from -6 to 6
- query_weight: bfloat16 [768, 768], replicated, may hold values from -0.21875 to 0.21875
- merge_weight: bfloat16 [768, 768], replicated, may hold values from -0.21875 to 0.21875
- image_lengths: int32 [64], P('rep'), parts along dimension 0, may hold values from 512 to 1024, as said below
- target_counts: int32 [128], P(('rep', 'tok')), parts along dimension 0, may hold values from 64 to 256, as said below
Outputs:
- tokens_out: bfloat16 [65536, 768], P(('rep', 'tok')), parts along dimension 0
- fast_updated: bfloat16 [3072, 2304], P(('rep', 'tok')), parts along dimension 0
- target_out: bfloat16 [32768, 768], P(('rep', 'tok')), parts along dimension 0
There are 4 independent parts, one for each index of `rep`. A program takes and returns all parts, laid end to end along the dimension named above; an argument that names none is the same for every part. Nothing has to cross between parts.
Inputs may be any that keep to these rules, and one draw needn't show every extreme that they name: `image_lengths`: every image has at least half of its 1024 slots valid, and some image of every scene is full. `target_counts`: some device of every scene uses all 256 slots. `head_temp`: positive score scales.
All inputs are finite; a program needn't handle non-finite values.
Results may differ from a plain program's by a relative error of at most 0.025.
The roundings to bfloat16 on the way count: a program that leaves them out, or rounds other values in their place, can miss the bound.
Values may be sent and summed in bfloat16 or wider, within the bound.
No kernel may reach another device: no remote copies, remote signals or barrier semaphores. Data moves between devices by JAX's collectives and lax.ppermute only.
A program may use at most 192 MiB of HBM per device.

v0:
```python
import jax
import jax.numpy as jnp
from jax import lax
from jax.sharding import PartitionSpec as P

eps = 1e-06
rate_base = 4.0


def partner(value, axis, bit):
    mask = 2**bit
    pairs = [(source, source ^ mask) for source in range(lax.axis_size(axis))]
    return lax.ppermute(value, axis, pairs)


def unit_rows(values):
    values = values.astype(jnp.float32)
    return values * lax.rsqrt(jnp.mean(values * values, axis=-1, keepdims=True) + eps)


def attend(query, keyset, valueset, temps, valid):
    head_dim = query.shape[-1]
    qhat = unit_rows(query).astype(jnp.bfloat16)
    khat = unit_rows(keyset).astype(jnp.bfloat16)
    scores = jnp.einsum("qhd,khd->hqk", qhat, khat, preferred_element_type=jnp.float32)
    scores = scores * (temps / head_dim)[:, None, None]
    scores = jnp.where(valid[None, None, :], scores, -1e30)
    top = jnp.max(scores, axis=-1, keepdims=True)
    expo = jnp.exp(scores - top)
    weights = (expo / jnp.sum(expo, axis=-1, keepdims=True)).astype(jnp.bfloat16)
    result = jnp.einsum("hqk,khd->qhd", weights, valueset, preferred_element_type=jnp.float32)
    return result.astype(jnp.bfloat16)


def rescale(start_rows, grad, fast_heads, fast_dim):
    count = start_rows.shape[0]
    start_w = start_rows.astype(jnp.float32).reshape(count, 3 * fast_heads, fast_dim)
    update = start_w - grad.reshape(count, 3 * fast_heads, fast_dim)
    fresh = (
        update
        * jnp.sqrt(jnp.mean(start_w * start_w, axis=-1, keepdims=True) + eps)
        * lax.rsqrt(jnp.mean(update * update, axis=-1, keepdims=True) + eps)
    )
    return fresh.reshape(count, 3 * fast_heads * fast_dim).astype(jnp.bfloat16)


def body(
    tokens,
    attn_gain,
    qkv_weight,
    head_temp,
    out_weight,
    kv_weight,
    rate_weight,
    fast_weights,
    target,
    query_weight,
    merge_weight,
    image_lengths,
    target_counts,
):
    tok_rows, width = tokens.shape
    devices = lax.axis_size("tok")
    place = lax.axis_index("tok")
    parity = place % 2
    heads = head_temp.shape[0]
    head_dim = width // heads
    half = heads // 2
    fast_hidden = fast_weights.shape[0]
    fast_heads = rate_weight.shape[1]
    fast_dim = width // fast_heads
    image_ids = jnp.arange(image_lengths.shape[0], dtype=jnp.int32)
    my_length = jnp.sum(jnp.where(image_ids == place // 2, image_lengths, 0))
    inputs = tokens.astype(jnp.float32)
    normed = (unit_rows(inputs) * attn_gain.astype(jnp.float32)).astype(jnp.bfloat16)
    qkv = jnp.dot(normed, qkv_weight, preferred_element_type=jnp.float32).astype(jnp.bfloat16)
    qkv = qkv.reshape(tok_rows, 3, heads, head_dim)
    key_valid = jnp.arange(2 * tok_rows, dtype=jnp.int32) < my_length
    leading = parity == 0
    owned = lax.dynamic_slice_in_dim(qkv, parity * half, half, 2)
    other = lax.dynamic_slice_in_dim(qkv, (1 - parity) * half, half, 2)
    arrived = partner(other.reshape(tok_rows, 3 * half * head_dim), "tok", 0)
    arrived = arrived.reshape(tok_rows, 3, half, head_dim)
    joined = jnp.concatenate(
        [jnp.where(leading, owned, arrived), jnp.where(leading, arrived, owned)], axis=0
    )
    temps = lax.dynamic_slice_in_dim(head_temp, parity * half, half, 0)
    result = attend(joined[:, 0], joined[:, 1], joined[:, 2], temps, key_valid)
    mine = jnp.where(leading, result[:tok_rows], result[tok_rows:])
    theirs = jnp.where(leading, result[tok_rows:], result[:tok_rows])
    returned = partner(theirs.reshape(tok_rows, half * head_dim), "tok", 0)
    returned = returned.reshape(tok_rows, half, head_dim)
    lower = jnp.where(leading, mine, returned)
    upper = jnp.where(leading, returned, mine)
    attn = jnp.concatenate([lower, upper], axis=1).reshape(tok_rows, width)
    tokens_out = (inputs + jnp.dot(attn, out_weight, preferred_element_type=jnp.float32)).astype(
        jnp.bfloat16
    )
    kv = jnp.dot(tokens_out, kv_weight, preferred_element_type=jnp.float32)
    own_valid = parity * tok_rows + jnp.arange(tok_rows, dtype=jnp.int32) < my_length
    logit = jnp.dot(tokens_out.astype(jnp.float32), rate_weight, precision=lax.Precision.HIGHEST)
    rate = (
        jax.nn.softplus(logit + 1.0)
        * (rate_base / (tok_rows * devices))
        * own_valid[:, None].astype(jnp.float32)
    )
    pieces = []
    for head in range(fast_heads):
        keys = unit_rows(kv[:, head * fast_dim : (head + 1) * fast_dim]).astype(jnp.bfloat16)
        values = kv[:, width + head * fast_dim : width + (head + 1) * fast_dim]
        base = 3 * head * fast_dim
        act_a = jnp.dot(
            keys, fast_weights[:, base : base + fast_dim].T, preferred_element_type=jnp.float32
        )
        act_b = jnp.dot(
            keys,
            fast_weights[:, base + fast_dim : base + 2 * fast_dim].T,
            preferred_element_type=jnp.float32,
        )
        hidden = (jax.nn.silu(act_a) * act_b).astype(jnp.bfloat16)
        push = (-rate[:, head : head + 1] * values).astype(jnp.bfloat16)
        back_h = jnp.dot(
            push,
            fast_weights[:, base + 2 * fast_dim : base + 3 * fast_dim].T,
            preferred_element_type=jnp.float32,
        )
        sigma = jax.nn.sigmoid(act_a)
        grad_a = (back_h * act_b * sigma * (1.0 + act_a * (1.0 - sigma))).astype(jnp.bfloat16)
        grad_b = (back_h * jax.nn.silu(act_a)).astype(jnp.bfloat16)
        pieces.append((keys, push, hidden, grad_a, grad_b))
    tq = jnp.dot(target, query_weight, preferred_element_type=jnp.float32)
    queries = [
        unit_rows(tq[:, head * fast_dim : (head + 1) * fast_dim]).astype(jnp.bfloat16)
        for head in range(fast_heads)
    ]
    rows = fast_hidden // devices
    blocks = []
    for keys, push, hidden, grad_a, grad_b in pieces:
        blocks.append(jnp.dot(grad_a.T, keys, preferred_element_type=jnp.float32))
        blocks.append(jnp.dot(grad_b.T, keys, preferred_element_type=jnp.float32))
        blocks.append(jnp.dot(hidden.T, push, preferred_element_type=jnp.float32))
    grad_mine = lax.psum_scatter(
        jnp.concatenate(blocks, axis=1).astype(jnp.bfloat16), "tok", scatter_dimension=0, tiled=True
    ).astype(jnp.float32)
    start_rows = lax.dynamic_slice_in_dim(fast_weights, place * rows, rows, 0)
    fresh = rescale(start_rows, grad_mine, fast_heads, fast_dim)
    piece = lax.all_gather(fresh, "tok", axis=0, tiled=True)
    results = []
    for apply_head in range(fast_heads):
        base = 3 * apply_head * fast_dim
        act_a = jnp.dot(
            queries[apply_head],
            piece[:, base : base + fast_dim].T,
            preferred_element_type=jnp.float32,
        )
        act_b = jnp.dot(
            queries[apply_head],
            piece[:, base + fast_dim : base + 2 * fast_dim].T,
            preferred_element_type=jnp.float32,
        )
        hidden_t = (jax.nn.silu(act_a) * act_b).astype(jnp.bfloat16)
        results.append(
            jnp.dot(
                hidden_t,
                piece[:, base + 2 * fast_dim : base + 3 * fast_dim],
                preferred_element_type=jnp.float32,
            )
        )
    outputs = jnp.stack(results, axis=0)
    fout = jnp.concatenate(
        [unit_rows(outputs[head]).astype(jnp.bfloat16) for head in range(fast_heads)], axis=1
    )
    merged = target.astype(jnp.float32) + jnp.dot(
        fout, merge_weight, preferred_element_type=jnp.float32
    )
    used = jnp.arange(target.shape[0], dtype=jnp.int32) < target_counts[0]
    target_out = jnp.where(used[:, None], merged, 0.0).astype(jnp.bfloat16)
    return (tokens_out, fresh, target_out)


def solution(mesh):
    placed = (
        P(("rep", "tok"), None),
        P(),
        P(),
        P(),
        P(),
        P(),
        P(),
        P(),
        P(("rep", "tok"), None),
        P(),
        P(),
        P("rep"),
        P(("rep", "tok")),
    )
    return jax.shard_map(
        body,
        mesh=mesh,
        in_specs=placed,
        out_specs=(P(("rep", "tok"), None), P(("rep", "tok"), None), P(("rep", "tok"), None)),
        check_vma=False,
    )
```

profile of v0, /device:TPU:0, one launch (start us, length us, event | category | flops | bytes accessed | tf_op | source)
XLA Modules:
  0.0 453.7 jit_solution(13452142345628719340)
XLA Ops:
  7.2 1.5 fusion.12
  9.5 4.6 %convolution_convert_fusion = bf16[512,2304]{1,0:T(8,128)(2,1)} fusion(bf16[768,2304]{1,0:T(8,128)(2,1)S(1)} %copy-done, bf16[512,768]{1,0:T(8,128)(2,1)} %param.13, f32[768]{0:T(1024)S(1)} %convert_element_type.114, f32[512]{0:T(512)S(1)} %add_rsqrt_fusion.5), kind=kOutput, calls=%fused_computation.9 | convolution fusion | flops 1814691840 | bytes 6689792 | tf_op jit(solution)/shard_map/dot_general | solution.py:76
  14.1 2.8 copy.24
  18.1 2.0 collective-permute-start
  21.5 24.8 %collective-permute-done = bf16[512,1152]{0,1:T(8,128)(2,1)S(1)} collective-permute-done((bf16[512,1152]{0,1:T(8,128)(2,1)}, bf16[512,1152]{0,1:T(8,128)(2,1)S(1)}, u32[]{:S(2)}, u32[]{:S(2)}) %collective-permute-start) | collective-permute-done | bytes 1179680 | tf_op jit(solution)/shard_map/ppermute | solution.py:13
  50.1 14.4 %fusion.117 = (f32[6,1024]{1,0:T(8,128)S(1)}, f32[6,1024,1024]{1,2,0:T(8,128)}) fusion(f32[6]{0:T(128)S(1)} %dynamic-slice_multiply_fusion, pred[1024]{0:T(1024)(128)(4,1)S(1)} %iota_compare_fusion, bf16[1024,6,64]{0,2,1:T(8,128)(2,1)} %get-tuple-element.25, f32[1024,6]{0,1:T(8,128)S(1)} %get-tuple-element.38, ...), kind=kOutput, calls=%fused_computation.172 | convolution fusion | flops 832832512 | bytes 26813464 | tf_op jit(solution)/shard_map/sub | solution.py:29
  64.5 9.4 %fusion.26 = bf16[1024,6,64]{0,2,1:T(8,128)(2,1)S(1)} fusion(f32[6,1024,1024]{1,2,0:T(8,128)} %get-tuple-element.33, f32[6,1024]{1,0:T(8,128)S(1)} %get-tuple-element.32, bf16[512,3,6,64]{0,3,2,1:T(8,128)(2,1)S(1)} %get-tuple-element.20, bf16[512,3,6,64]{0,3,2,1:T(8,128)(2,1)S(1)} %copy-done.3), kind=kOutput, calls=%fused_computation.59 | convolution fusion | flops 819855360 | bytes 28336128 | tf_op jit(solution)/shard_map/hqk,khd->qhd/dot_general | solution.py:31
  74.0 2.0 collective-permute-start.1
  76.7 7.9 %collective-permute-done.1 = bf16[512,384]{0,1:T(8,128)(2,1)S(1)} collective-permute-done((bf16[512,384]{0,1:T(8,128)(2,1)S(1)}, bf16[512,384]{0,1:T(8,128)(2,1)S(1)}, u32[]{:S(2)}, u32[]{:S(2)}) %collective-permute-start.1) | collective-permute-done | bytes 393248 | tf_op jit(solution)/shard_map/ppermute | solution.py:13
  89.6 1.5 copy-done.4
  95.6 1.8 fusion.24
  97.3 1.6 fusion.23
  98.9 1.6 fusion.22
  100.5 1.8 fusion.21
  102.3 1.6 fusion.20
  103.9 1.6 fusion.19
  105.5 5.8 %copy.30 = bf16[768,2304]{1,0:T(8,128)(2,1)} copy(bf16[768,2304]{0,1:T(8,128)(2,1)} %fusion.19) | data formatting | bytes 7077888
  113.5 166.8 %reduce-scatter.4.cloned.1.call-done = bf16[24,2304]{1,0:T(8,128)(2,1)} async-done(((bf16[768,2304]{1,0:T(8,128)(2,1)}), bf16[24,2304]{1,0:T(8,128)(2,1)}) %reduce-scatter.4.cloned.1.call-update) | async-done | bytes 110608
  284.5 150.8 %all-gather.2.cloned.1.call-done = bf16[768,2304]{1,0:T(8,128)(2,1)} async-done(((bf16[24,2304]{1,0:T(8,128)(2,1)}), bf16[768,2304]{1,0:T(8,128)(2,1)}) %all-gather.2.cloned.1.call-update) | async-done | bytes 3538960 | tf_op jit(solution)/shard_map/all_gather | solution.py:147
  435.2 1.5 fusion.74
  436.7 2.0 multiply_reduce_fusion.4
  438.7 1.5 fusion.69
  440.2 2.7 multiply_reduce_fusion.2
  444.3 2.6 fusion.27
  (78 shorter events, 24.0 us)
Async XLA Ops:
  7.2 2.3 copy-start
  7.2 273.2 %reduce-scatter.4.cloned.1.call-start = ((), (), s32[]{:S(2)}) async-start(), calls=%async_computation.2 | async-start | bytes 3649536
  16.9 3.1 copy-start.13
  16.9 3.2 copy-start.14
  18.1 28.2 %collective-permute-start = (bf16[512,1152]{0,1:T(8,128)(2,1)}, bf16[512,1152]{0,1:T(8,128)(2,1)S(1)}, u32[]{:S(2)}, u32[]{:S(2)}) collective-permute-start(bf16[512,1152]{0,1:T(8,128)(2,1)} %bitcast.1), channel_id=1, source_target_pairs={{0,4},{4,0},{8,12},{12,8},{16,20},{20,16},{24,28},{28,24},{32,36},... | collective-permute-start | bytes 3538952 | tf_op jit(solution)/shard_map/ppermute | solution.py:13
  46.3 1.0 copy-start.5
  48.7 1.3 copy-start.2
  50.0 14.4 %copy-start.3 = (bf16[512,3,6,64]{0,3,2,1:T(8,128)(2,1)S(1)}, bf16[512,3,6,64]{0,3,2,1:T(8,128)(2,1)}, u32[]{:S(2)}) copy-start(bf16[512,3,6,64]{0,3,2,1:T(8,128)(2,1)} %copy-done.2) | copy-start | bytes 3538948
  74.0 10.5 %collective-permute-start.1 = (bf16[512,384]{0,1:T(8,128)(2,1)S(1)}, bf16[512,384]{0,1:T(8,128)(2,1)S(1)}, u32[]{:S(2)}, u32[]{:S(2)}) collective-permute-start(bf16[512,384]{0,1:T(8,128)(2,1)S(1)} %bitcast.59), channel_id=1, source_target_pairs={{0,4},{4,0},{8,12},{12,8},{16,20},{20,16},{24,28},{28,24},{32,36},... | collective-permute-start | bytes 1179656 | tf_op jit(solution)/shard_map/ppermute | solution.py:13
  84.5 1.1 copy-start.7
  84.5 1.5 copy-start.12
  86.0 1.7 copy-start.11
  87.7 5.8 %copy-start.8 = (bf16[512,768]{1,0:T(8,128)(2,1)}, bf16[512,768]{1,0:T(8,128)(2,1)S(1)}, u32[]{:S(2)}) copy-start(bf16[512,768]{1,0:T(8,128)(2,1)S(1)} %fusion.15) | copy-start | bytes 2359300
  89.1 2.0 copy-start.4
  92.9 0.7 copy-start.10
  111.3 323.9 %all-gather.2.cloned.1.call-start = ((), (), s32[]{:S(2)}) async-start(), calls=%async_computation.1 | async-start | bytes 3649536 | tf_op jit(solution)/shard_map/all_gather | solution.py:147
  282.0 1.8 copy-start.6
  282.0 1.8 copy-start.9
  443.0 3.9 copy-start.1
Sparse Core Ops, SparseCore 0:
  111.5 168.8 reduce-scatter.3
  283.3 151.9 all-gather.1
where the time goes:
time: 454 us
  waiting for transfers between devices  350 us (77%)
  matrix products  55.7 us (12%)
  local copies, waits for them, and re-layouts  18.6 us (4%)
  between operations  15.1 us (3%)
  other arithmetic  9.74 us (2%)
    unnamed x3, waiting for transfers between devices  167 us
    all_gather x1, waiting for transfers between devices, body(): piece = lax.all_gather(fresh, 'tok', axis=0, tiled=True)  151 us
    ppermute x2, waiting for transfers between devices, partner(): return lax.ppermute(value, axis, pairs)  32.7 us
    sub x1, matrix products, attend(): expo = jnp.exp(scores - top)  14.4 us
    unnamed x34, local copies, waits for them, and re-layouts  14 us
    dot_general x1, matrix products, attend(): jnp.einsum('hqk,khd->qhd', weights, valueset, preferred_element_type=jnp....  9.44 us
  transfers between devices with their start and end apart: 4, of which 4 were waited for; matrix products, arithmetic and copies ran while one was open for 1% of the time, Pallas kernels for 0%

commit v1 on v0

v1 whole, which is shorter than its diff:
```python
import functools
import math

import jax
import jax.numpy as jnp
from jax import lax
from jax.experimental import pallas as pl
from jax.experimental.pallas import tpu as pltpu
from jax.sharding import PartitionSpec as P

eps = 1e-06
rate_base = 4.0
safe_temp = 60.0
bf16 = jnp.bfloat16
f32 = jnp.float32

pair_mask = 1
reduce_orders = ((3, 4, 8, 24), (8, 24, 3, 4))


def swap(value, mask):
    pairs = [(source, source ^ mask) for source in range(lax.axis_size("tok"))]
    return lax.ppermute(value, "tok", pairs)


def params(mib, *semantics):
    return pltpu.CompilerParams(vmem_limit_bytes=mib * 2**20)


def nn(a, b):
    return lax.dot_general(a, b, (((1,), (0,)), ((), ())), preferred_element_type=f32)


def nt(a, b):
    return lax.dot_general(a, b, (((1,), (1,)), ((), ())), preferred_element_type=f32)


def whole(shape):
    return pl.BlockSpec(shape, lambda *_: (0,) * len(shape))


smem = pl.BlockSpec(memory_space=pltpu.SMEM)


def gather_kernel(index_ref, rows_ref, out_ref, sems):
    copies = []
    heads, blocks = index_ref.shape
    width = out_ref.shape[-1]
    for head in range(heads):
        for block in range(blocks):
            copies.append(
                pltpu.make_async_copy(
                    rows_ref.at[index_ref[head, block], :, pl.ds(head * width, width)],
                    out_ref.at[head, block],
                    sems.at[head, block],
                )
            )
    for copy in copies:
        copy.start()
    for copy in copies:
        copy.wait()


def gather_rows(index, rows):
    heads, blocks = index.shape
    _, height, width = rows.shape
    return pl.pallas_call(
        gather_kernel,
        out_shape=jax.ShapeDtypeStruct((heads, blocks, height, width // heads), rows.dtype),
        in_specs=[smem, pl.BlockSpec(memory_space=pl.ANY)],
        out_specs=pl.BlockSpec(memory_space=pl.ANY),
        scratch_shapes=[pltpu.SemaphoreType.DMA((heads, blocks))],
        name="gather_rows",
    )(index, rows)


def qkv_kernel(valid_ref, tok_ref, gain_ref, scale_ref, wq_ref, wk_ref, wv_ref, q_ref, k_ref, v_ref, normed):
    @pl.when(pl.program_id(0) == 0)
    def _():
        x = tok_ref[...].astype(f32)
        unit = x * lax.rsqrt(jnp.mean(x * x, axis=-1, keepdims=True) + eps)
        normed[...] = (unit * gain_ref[...].astype(f32)).astype(bf16)

    rows = normed[...]
    count, cols = q_ref.shape[0], wq_ref.shape[1]
    low = lax.broadcasted_iota(jnp.int32, (count, 128), 1) < 64
    same = lax.broadcasted_iota(jnp.int32, (cols, cols), 0) >> 6 == lax.broadcasted_iota(jnp.int32, (cols, cols), 1) >> 6
    ones = jnp.where(same, 1.0, 0.0).astype(bf16)

    def unit_heads(t):
        square = t * t
        high = square.astype(bf16)
        rest = (square - high.astype(f32)).astype(bf16)
        total = nn(high, ones) + nn(rest, ones)
        return (t * lax.rsqrt(total * (1.0 / 64.0) + eps)).astype(bf16).astype(f32)

    query = unit_heads(nn(rows, wq_ref[...]).astype(bf16).astype(f32)) * scale_ref[...]
    q_high = query.astype(bf16).astype(f32)
    q_rest = query - q_high
    key = unit_heads(nn(rows, wk_ref[...]).astype(bf16).astype(f32))
    value = nn(rows, wv_ref[...])
    live = lax.broadcasted_iota(jnp.int32, (count, 128), 0) < valid_ref[0]
    for tile in range(cols // 128):
        part = slice(tile * 128, tile * 128 + 128)
        even = slice(tile * 256, tile * 256 + 128)
        odd = slice(tile * 256 + 128, tile * 256 + 256)
        moved = pltpu.roll(q_rest[:, part], 64, 1)
        q_ref[:, even] = jnp.where(low, q_high[:, part], moved).astype(bf16)
        q_ref[:, odd] = jnp.where(low, moved, q_high[:, part]).astype(bf16)
        moved = pltpu.roll(key[:, part], 64, 1)
        k_ref[:, even] = jnp.where(low, key[:, part], moved).astype(bf16)
        k_ref[:, odd] = jnp.where(low, moved, key[:, part]).astype(bf16)
        shown = jnp.where(live, value[:, part], 0.0)
        one = jnp.where(live, 1.0, 0.0)
        v_ref[:, even] = jnp.where(low, shown, one).astype(bf16)
        v_ref[:, odd] = jnp.where(low, one, shown).astype(bf16)


def project_qkv(valid, tokens, gain, scale, weight):
    count, width = tokens.shape
    cols = 256
    steps = width // cols
    out = jax.ShapeDtypeStruct((count, 2 * width), bf16)
    return pl.pallas_call(
        qkv_kernel,
        grid=(steps,),
        out_shape=(out, out, out),
        in_specs=[
            smem,
            whole((count, width)),
            whole((1, width)),
            pl.BlockSpec((1, cols), lambda i: (0, i)),
            pl.BlockSpec((width, cols), lambda i: (0, i)),
            pl.BlockSpec((width, cols), lambda i: (0, steps + i)),
            pl.BlockSpec((width, cols), lambda i: (0, 2 * steps + i)),
        ],
        out_specs=[pl.BlockSpec((count, 2 * cols), lambda i: (0, i))] * 3,
        scratch_shapes=[pltpu.VMEM((count, width), bf16)],
        compiler_params=params(32),
        name="project_qkv",
    )(valid, tokens, gain, scale, weight, weight, weight)


def attend_kernel(valid_ref, temp_ref, q0_ref, q1_ref, k0_ref, k1_ref, v0_ref, v1_ref, out_ref):
    pair = pl.program_id(0)
    count = q0_ref.shape[0]
    block = 256
    low = lax.broadcasted_iota(jnp.int32, (block, 128), 1) < 64
    spot = lax.broadcasted_iota(jnp.int32, (block, count), 1)

    def fill(weigh):
        for side, q_ref in enumerate((q0_ref, q1_ref)):
            for first in range(0, count, block):
                sums = []
                for head in range(2):
                    lanes = slice(head * 128, head * 128 + 128)
                    q = q_ref[first : first + block, lanes]
                    p0, p1 = weigh(nt(q, k0_ref[:, lanes]), nt(q, k1_ref[:, lanes]))
                    sums.append(nn(p0, v0_ref[:, lanes]) + nn(p1, v1_ref[:, lanes]))
                top = jnp.where(low, sums[0], sums[1])
                bottom = pltpu.roll(jnp.where(low, sums[1], sums[0]), 64, 1)
                start = side * count + first
                out_ref[start : start + block, :] = (top / bottom).astype(bf16)

    plain = jnp.maximum(temp_ref[2 * pair], temp_ref[2 * pair + 1]) <= safe_temp

    @pl.when(plain)
    def _():
        fill(lambda s0, s1: (jnp.exp2(s0).astype(bf16), jnp.exp2(s1).astype(bf16)))

    @pl.when(jnp.logical_not(plain))
    def _():
        def weigh(s0, s1):
            s0 = jnp.where(spot < valid_ref[0], s0, -1e30)
            s1 = jnp.where(spot < valid_ref[1], s1, -1e30)
            top = jnp.max(jnp.maximum(s0, s1), axis=-1, keepdims=True)
            return jnp.exp2(s0 - top).astype(bf16), jnp.exp2(s1 - top).astype(bf16)

        fill(weigh)


def attend(valid, temps, q0, q1, k0, k1, v0, v1):
    count, width = q0.shape
    block = pl.BlockSpec((count, 256), lambda i: (0, i))
    return pl.pallas_call(
        attend_kernel,
        grid=(width // 256,),
        out_shape=jax.ShapeDtypeStruct((2 * count, width // 2), bf16),
        in_specs=[smem, smem] + [block] * 6,
        out_specs=pl.BlockSpec((2 * count, 128), lambda i: (0, i)),
        compiler_params=params(32),
        name="attend",
    )(valid, temps, q0, q1, k0, k1, v0, v1)


def push_kernel(scale, valid_ref, attn_ref, t0_ref, t1_ref, wo_ref, wkv_ref, r0_ref, r1_ref, r2_ref, out_ref, key_ref, push_ref):
    side = pl.program_id(0)
    count, width = t0_ref.shape
    before = jnp.where(side == 0, t0_ref[...], t1_ref[...]).astype(f32)
    after = (before + nn(attn_ref[...], wo_ref[...])).astype(bf16)

    @pl.when(side == 0)
    def _():
        out_ref[...] = after

    kv = nn(after, wkv_ref[...])
    logit = nn(after, r0_ref[...]) + nn(after, r1_ref[...]) + nn(after, r2_ref[...])
    high = logit + 1.0
    soft = jnp.maximum(high, 0.0) + jnp.log1p(jnp.exp(-jnp.abs(high)))
    live = lax.broadcasted_iota(jnp.int32, logit.shape, 0) < valid_ref[side]
    rate = jnp.where(live, soft * scale, 0.0)
    heads = logit.shape[1] // 128
    size = width // heads
    for head in range(heads):
        part = slice(head * size, head * size + size)
        key = kv[:, part]
        inv = lax.rsqrt(jnp.mean(key * key, axis=-1, keepdims=True) + eps)
        key_ref[:, part] = (key * inv).astype(bf16)
        for tile in range(size // 128):
            at = head * size + tile * 128
            value = kv[:, width + at : width + at + 128]
            push_ref[:, at : at + 128] = (-rate[:, head * 128 : head * 128 + 128] * value).astype(bf16)


def make_pushes(scale, valid, attn, t0, t1, wo, wkv, rates):
    count, width = t0.shape
    both = jax.ShapeDtypeStruct((2 * count, width), bf16)
    block = pl.BlockSpec((count, width), lambda i: (i, 0))
    return pl.pallas_call(
        functools.partial(push_kernel, scale),
        grid=(2,),
        out_shape=(jax.ShapeDtypeStruct((count, width), bf16), both, both),
        in_specs=[
            smem,
            block,
            whole((count, width)),
            whole((count, width)),
            whole(wo.shape),
            whole(wkv.shape),
        ]
        + [whole(rates[0].shape)] * 3,
        out_specs=[whole((count, width)), block, block],
        compiler_params=params(40),
        name="make_pushes",
    )(valid, attn, t0, t1, wo, wkv, *rates)


def grad_kernel(w_ref, key_ref, push_ref, out_ref):
    size = key_ref.shape[1]
    key, push = key_ref[...], push_ref[...]
    act_a = nt(w_ref[0, :, :size], key)
    act_b = nt(w_ref[0, :, size : 2 * size], key)
    back = nt(w_ref[0, :, 2 * size :], push)
    sigma = 1.0 / (1.0 + jnp.exp(-act_a))
    silu = act_a * sigma
    hidden = (silu * act_b).astype(bf16)
    grad_a = (back * act_b * sigma * (1.0 + act_a * (1.0 - sigma))).astype(bf16)
    grad_b = (back * silu).astype(bf16)
    out_ref[:, :size] = nn(grad_a, key).astype(out_ref.dtype)
    out_ref[:, size : 2 * size] = nn(grad_b, key).astype(out_ref.dtype)
    out_ref[:, 2 * size :] = nn(hidden, push).astype(out_ref.dtype)


def gradient(weights, keys, pushes, head, half, kind):
    _, rows, cols = weights.shape
    count = keys.shape[0]
    size = cols // 3
    column = pl.BlockSpec((count, size), lambda i: (0, head))
    return pl.pallas_call(
        grad_kernel,
        grid=(1,),
        out_shape=jax.ShapeDtypeStruct((rows // 2, cols), kind),
        in_specs=[pl.BlockSpec((1, rows // 2, cols), lambda i: (head, half, 0)), column, column],
        out_specs=whole((rows // 2, cols)),
        compiler_params=params(32),
        name="gradient",
    )(weights, keys, pushes)


def rescale_kernel(start_ref, mine_ref, theirs_ref, out_ref):
    size = start_ref.shape[1] // 3
    grad = mine_ref[...] + theirs_ref[...].astype(f32)
    for block in range(3):
        part = slice(block * size, block * size + size)
        start = start_ref[:, part].astype(f32)
        update = start - grad[:, part]
        before = jnp.sqrt(jnp.mean(start * start, axis=-1, keepdims=True) + eps)
        after = lax.rsqrt(jnp.mean(update * update, axis=-1, keepdims=True) + eps)
        out_ref[:, part] = (update * before * after).astype(bf16)


def rescale(start, mine, theirs):
    return pl.pallas_call(
        rescale_kernel,
        grid=(1,),
        out_shape=jax.ShapeDtypeStruct(start.shape, bf16),
        in_specs=[whole(start.shape)] * 3,
        out_specs=whole(start.shape),
        compiler_params=params(8),
        name="rescale",
    )(start, mine, theirs)


def query_kernel(t0_ref, t1_ref, w_ref, out_ref):
    side = pl.program_id(0)
    width = t0_ref.shape[1]
    size = width // 2
    tq = nn(jnp.where(side == 0, t0_ref[...], t1_ref[...]), w_ref[...])
    for head in range(2):
        part = slice(head * size, head * size + size)
        q = tq[:, part]
        out_ref[:, part] = (q * lax.rsqrt(jnp.mean(q * q, axis=-1, keepdims=True) + eps)).astype(bf16)


def target_queries(t0, t1, weight):
    count, width = t0.shape
    return pl.pallas_call(
        query_kernel,
        grid=(2,),
        out_shape=jax.ShapeDtypeStruct((2 * count, width), bf16),
        in_specs=[whole((count, width))] * 2 + [whole(weight.shape)],
        out_specs=pl.BlockSpec((count, width), lambda i: (i, 0)),
        compiler_params=params(16),
        name="target_queries",
    )(t0, t1, weight)


def apply_rows(q, w_ref):
    size = q.shape[1]
    act_a = nt(q, w_ref[:, :size])
    act_b = nt(q, w_ref[:, size : 2 * size])
    hidden = (act_a / (1.0 + jnp.exp(-act_a)) * act_b).astype(bf16)
    return nn(hidden, w_ref[:, 2 * size :])


def first_kernel(q_ref, w_ref, out_ref):
    out_ref[...] = apply_rows(q_ref[...], w_ref)


def apply_first(queries, weights, head):
    count = queries.shape[0]
    size = weights.shape[1] // 3
    return pl.pallas_call(
        first_kernel,
        grid=(1,),
        out_shape=jax.ShapeDtypeStruct((count, size), f32),
        in_specs=[pl.BlockSpec((count, size), lambda i: (0, head)), whole(weights.shape)],
        out_specs=whole((count, size)),
        compiler_params=params(16),
        name="apply_first",
    )(queries, weights)


def last_kernel(q_ref, w_ref, sum_ref, mine_ref, theirs_ref):
    count = mine_ref.shape[0]
    total = sum_ref[...] + apply_rows(q_ref[...], w_ref)
    mine_ref[...] = total[:count]
    theirs_ref[...] = total[count:].astype(bf16)


def apply_last(queries, weights, total, head):
    count = queries.shape[0]
    size = weights.shape[1] // 3
    return pl.pallas_call(
        last_kernel,
        grid=(1,),
        out_shape=(
            jax.ShapeDtypeStruct((count // 2, size), f32),
            jax.ShapeDtypeStruct((count // 2, size), bf16),
        ),
        in_specs=[
            pl.BlockSpec((count, size), lambda i: (0, head)),
            whole(weights.shape),
            whole((count, size)),
        ],
        out_specs=[whole((count // 2, size))] * 2,
        compiler_params=params(16),
        name="apply_last",
    )(queries, weights, total)


def merge_kernel(used_ref, target_ref, w_ref, m0_ref, m1_ref, r0_ref, r1_ref, out_ref):
    size = m0_ref.shape[1]
    total = target_ref[...].astype(f32)
    for head, (mine, theirs) in enumerate(((m0_ref, r0_ref), (m1_ref, r1_ref))):
        fout = mine[...] + theirs[...].astype(f32)
        unit = (fout * lax.rsqrt(jnp.mean(fout * fout, axis=-1, keepdims=True) + eps)).astype(bf16)
        total = total + nn(unit, w_ref[head * size : head * size + size, :])
    live = lax.broadcasted_iota(jnp.int32, total.shape, 0) < used_ref[0]
    out_ref[...] = jnp.where(live, total, 0.0).astype(bf16)


def merge(used, target, weight, mine, theirs):
    return pl.pallas_call(
        merge_kernel,
        grid=(1,),
        out_shape=jax.ShapeDtypeStruct(target.shape, bf16),
        in_specs=[smem, whole(target.shape), whole(weight.shape)] + [whole(mine[0].shape)] * 4,
        out_specs=whole(target.shape),
        compiler_params=params(16),
        name="merge",
    )(used, target, weight, *mine, *theirs)


def split_weight(value):
    parts = []
    for _ in range(3):
        part = lax.reduce_precision(value, 8, 7)
        parts.append(part.astype(bf16))
        value = value - part
    return parts


def body(
    tokens,
    attn_gain,
    qkv_weight,
    head_temp,
    out_weight,
    kv_weight,
    rate_weight,
    fast_weights,
    target,
    query_weight,
    merge_weight,
    image_lengths,
    target_counts,
):
    tok_rows, width = tokens.shape
    devices = lax.axis_size("tok")
    place = lax.axis_index("tok")
    parity = place % 2
    head_dim = width // head_temp.shape[0]
    fast_hidden, fast_cols = fast_weights.shape
    fast_heads = rate_weight.shape[1]
    rows = fast_hidden // devices
    image_ids = jnp.arange(image_lengths.shape[0], dtype=jnp.int32)
    length = jnp.sum(jnp.where(image_ids == place // 2, image_lengths, 0))
    valid = jnp.stack([length - parity * tok_rows, length - (1 - parity) * tok_rows]).astype(jnp.int32)

    arrived = swap(tokens, pair_mask)

    scale = jnp.repeat(head_temp * (math.log2(math.e) / head_dim), head_dim)[None, :]
    gain = attn_gain[None, :]
    q0, k0, v0 = project_qkv(valid[:1], tokens, gain, scale, qkv_weight)

    moves = []
    for order in reduce_orders:
        span = [0]
        for mask in reversed(order):
            span = span + [mask ^ at for at in span]
        moves.append(span)
    index = place ^ jnp.array(moves, dtype=jnp.int32)
    start = gather_rows(index, fast_weights.reshape(devices, rows, fast_cols))
    weights = start.reshape(fast_heads, len(moves[0]) * rows, fast_cols // fast_heads)
    rates = [
        jnp.broadcast_to(part[:, :, None], part.shape + (128,)).reshape(width, fast_heads * 128)
        for part in split_weight(rate_weight)
    ]

    arrived, target_sent = lax.optimization_barrier((arrived, target))
    other_target = swap(target_sent, pair_mask)
    q1, k1, v1 = project_qkv(valid[1:], arrived, gain, scale, qkv_weight)
    attn = attend(valid, head_temp, q0, q1, k0, k1, v0, v1)
    tokens_out, keys, pushes = make_pushes(
        rate_base / (tok_rows * devices), valid, attn, tokens, arrived, out_weight, kv_weight, rates
    )

    sent = [gradient(weights, keys, pushes, head, 1, bf16) for head in range(fast_heads)]
    kept = [gradient(weights, keys, pushes, head, 0, f32) for head in range(fast_heads)]
    for step in range(len(reduce_orders[0])):
        got = [swap(sent[head], reduce_orders[head][step]) for head in range(fast_heads)]
        if step < len(reduce_orders[0]) - 1:
            half = kept[0].shape[0] // 2
            total = [kept[head] + got[head].astype(f32) for head in range(fast_heads)]
            kept = [part[:half] for part in total]
            sent = [part[half:].astype(bf16) for part in total]
    fresh = [rescale(start[head, 0], kept[head], got[head]) for head in range(fast_heads)]

    queries = target_queries(target, other_target, query_weight)
    held = list(fresh)
    steps = len(reduce_orders[0])
    for step in range(steps - 1):
        got = [swap(held[head], reduce_orders[head][steps - 1 - step]) for head in range(fast_heads)]
        held = [jnp.concatenate([held[head], got[head]], axis=0) for head in range(fast_heads)]
    got = [swap(held[head], reduce_orders[head][0]) for head in range(fast_heads)]
    mine, theirs = [], []
    totals = [apply_first(queries, held[head], head) for head in range(fast_heads)]
    for head in range(fast_heads):
        own, other = apply_last(queries, got[head], totals[head], head)
        mine.append(own)
        theirs.append(swap(other, pair_mask))
    target_out = merge(target_counts, target, merge_weight, mine, theirs)
    return (tokens_out, jnp.concatenate(fresh, axis=1), target_out)


def solution(mesh):
    placed = (
        P(("rep", "tok"), None),
        P(),
        P(),
        P(),
        P(),
        P(),
        P(),
        P(),
        P(("rep", "tok"), None),
        P(),
        P(),
        P("rep"),
        P(("rep", "tok")),
    )
    return jax.shard_map(
        body,
        mesh=mesh,
        in_specs=placed,
        out_specs=(P(("rep", "tok"), None), P(("rep", "tok"), None), P(("rep", "tok"), None)),
        check_vma=False,
    )
```

time: 454 us -> 202 us (0.44)
  waiting for transfers between devices: 350 us -> 37.4 us
  Pallas kernels: 0 us -> 117 us
  matrix products: 55.7 us -> 0 us
  starting transfers between devices: 4.31 us -> 31.8 us
  between operations: 15.1 us -> 3.01 us
  local copies, waits for them, and re-layouts: 18.6 us -> 7.88 us
  other arithmetic: 9.74 us -> 4.36 us
    unnamed x3 -> x0, waiting for transfers between devices: 167 us -> none
    all_gather x1 -> x0, waiting for transfers between devices: 151 us -> none  [body(): piece = lax.all_gather(fresh, 'tok', axis=0, tiled=True)]
    pallas_call x0 -> x17, Pallas kernels: none -> 117 us  [the longest x1 55.8 us: gather_rows(): pl.pallas_call(gather_kernel, out_shape=jax.ShapeDtypeStruct((heads, bloc...]
    dot_general x23 -> x0, matrix products: 41.2 us -> none  [the longest x1 9.44 us: attend(): jnp.einsum('hqk,khd->qhd', weights, valueset, preferred_element_type=jnp....]
    ppermute x2 -> x20, starting transfers between devices: 4.01 us -> 31.8 us  [swap(): return lax.ppermute(value, 'tok', pairs)]
    sub x1 -> x0, matrix products: 14.4 us -> none  [attend(): expo = jnp.exp(scores - top)]
    unnamed x34 -> x29, local copies, waits for them, and re-layouts: 14 us -> 2.01 us
    ppermute x2 -> x20, waiting for transfers between devices: 32.7 us -> 37.4 us  [swap(): return lax.ppermute(value, 'tok', pairs)]
  transfers between devices with their start and end apart: 4 -> 20, of which waited for: 4 -> 14; matrix products, arithmetic and copies ran while one was open for 1% -> 5% of each run, Pallas kernels for 0% -> 35%
where the time goes in v1:
time: 202 us; the launch traced here: 201 us
  Pallas kernels  117 us (58%)
  waiting for transfers between devices  37.4 us (19%)
  starting transfers between devices  31.8 us (16%)
  local copies, waits for them, and re-layouts  7.88 us (4%)
  other arithmetic  4.36 us (2%)
  between operations  3.01 us (1%)
    pallas_call x1, Pallas kernels, gather_rows(): pl.pallas_call(gather_kernel, out_shape=jax.ShapeDtypeStruct((heads, bloc...  55.8 us
    ppermute x20, waiting for transfers between devices, swap(): return lax.ppermute(value, 'tok', pairs)  37.4 us
    ppermute x20, starting transfers between devices, swap(): return lax.ppermute(value, 'tok', pairs)  31.8 us
    pallas_call x1, Pallas kernels, attend(): pl.pallas_call(attend_kernel, grid=(width // 256,), out_shape=jax.ShapeDt...  24.8 us
    pallas_call x2, Pallas kernels, project_qkv(): pl.pallas_call(qkv_kernel, grid=(steps,), out_shape=(out, out, out), in_s...  13.4 us
    pallas_call x1, Pallas kernels, make_pushes(): pl.pallas_call(functools.partial(push_kernel, scale), grid=(2,), out_shap...  10 us
    pallas_call x4, Pallas kernels, gradient(): pl.pallas_call(grad_kernel, grid=(1,), out_shape=jax.ShapeDtypeStruct((ro...  7.29 us
  transfers between devices with their start and end apart: 20, of which 14 were waited for; matrix products, arithmetic and copies ran while one was open for 5% of the time, Pallas kernels for 35%

profile of v1, /device:TPU:0, one launch (start us, length us, event | category | flops | bytes accessed | tf_op | source)
XLA Modules:
  0.0 200.9 jit_solution(4984532782372522770)
XLA Ops:
  0.6 2.1 %collective-permute-start = (bf16[512,768]{1,0:T(8,128)(2,1)}, bf16[512,768]{1,0:T(8,128)(2,1)}, u32[]{:S(2)}, u32[]{:S(2)}) collective-permute-start(bf16[512,768]{1,0:T(8,128)(2,1)} %t0_ref.2), channel_id=1, source_target_pairs={{0,4},{4,0},{8,12},{12,8},{16,20},{20,16},{24,28},{28,24},{32,36},... | collective-permute-start | bytes 2359304 | tf_op jit(solution)/shard_map/ppermute | solution.py:23
  11.8 55.8 %gather_rows.1 = bf16[2,16,24,1152]{3,2,1,0:T(8,128)(2,1)} custom-call(s32[2,16]{1,0:T(2,128)} %broadcast_xor_fusion.index_ref, bf16[32,24,2304]{2,1,0:T(8,128)(2,1)} %bitcast.23), custom_call_target="tpu_custom_call" | custom-call | tf_op jit(solution)/shard_map/gather_rows/pallas_call | solution.py:67
  68.7 6.1 %project_qkv.2 = (bf16[512,1536]{1,0:T(8,128)(2,1)S(1)}, bf16[512,1536]{1,0:T(8,128)(2,1)S(1)}, bf16[512,1536]{1,0:T(8,128)(2,1)S(1)}) custom-call(s32[1]{0:T(128)} %bitcast.valid_ref, bf16[512,768]{1,0:T(8,128)(2,1)S(1)} %copy-done.2, bf16[1,768]{1,0:T(2,128)(2,1)S(1)} %broadcast_in_dim.15.gain_ref, f32[1,768]{1,0:T(1,128)S(1)} %broadcast_in_dim_reshape.3.scale_ref, ...), custom_call_target="tpu_custom_call" | custom-call | tf_op jit(solution)/shard_map/project_qkv/pallas_call | solution.py:124
  77.1 7.2 %project_qkv.3 = (bf16[512,1536]{1,0:T(8,128)(2,1)S(1)}, bf16[512,1536]{1,0:T(8,128)(2,1)S(1)}, bf16[512,1536]{1,0:T(8,128)(2,1)S(1)}) custom-call(s32[1]{0:T(128)} %bitcast.1.valid_ref, bf16[512,768]{1,0:T(8,128)(2,1)} %collective-permute-done.tok_ref.t1_ref, bf16[1,768]{1,0:T(2,128)(2,1)S(1)} %broadcast_in_dim.15.gain_ref, ...), custom_call_target="tpu_custom_call" | custom-call | tf_op jit(solution)/shard_map/project_qkv/pallas_call | solution.py:124
  84.4 24.8 %attend.1.attn_ref = bf16[1024,768]{1,0:T(8,128)(2,1)S(1)} custom-call(s32[2]{0:T(128)S(1)} %pad_add_fusion.valid_ref, f32[12]{0:T(128)S(1)} %copy-done.10, bf16[512,1536]{1,0:T(8,128)(2,1)S(1)} %get-tuple-element.18.q0_ref, bf16[512,1536]{1,0:T(8,128)(2,1)S(1)} %get-tuple-element.20.q1_ref, bf16[512,1536]{1,0:T(8,128)(2,1)S(1)} %get-tuple-element.21.k0_ref, ...), custom_call_target="tpu_custom_call" | custom-call | tf_op jit(solution)/shard_map/attend/pallas_call | solution.py:185
  109.2 10.0 %make_pushes.1 = (bf16[512,768]{1,0:T(8,128)(2,1)}, bf16[1024,768]{1,0:T(8,128)(2,1)S(1)}, bf16[1024,768]{1,0:T(8,128)(2,1)S(1)}) custom-call(s32[2]{0:T(128)S(1)} %pad_add_fusion.valid_ref, bf16[1024,768]{1,0:T(8,128)(2,1)S(1)} %attend.1.attn_ref, bf16[512,768]{1,0:T(8,128)(2,1)S(1)} %copy-done.3, bf16[512,768]{1,0:T(8,128)(2,1)} %collective-permute-done.tok_ref.t1_ref, ...), custom_call_target="tpu_custom_call" | custom-call | tf_op jit(solution)/shard_map/make_pushes/pallas_call | solution.py:229
  121.1 1.9 collective-permute-start.5
  124.8 1.8 gradient.5
  128.5 2.6 %collective-permute-start.1 = (bf16[192,1152]{1,0:T(8,128)(2,1)S(1)}, bf16[192,1152]{1,0:T(8,128)(2,1)S(1)}, u32[]{:S(2)}, u32[]{:S(2)}) collective-permute-start(bf16[192,1152]{1,0:T(8,128)(2,1)S(1)} %gradient.5), channel_id=1, source_target_pairs={{0,12},{4,8},{8,4},{12,0},{16,28},{20,24},{24,20},{28,16},{32,44},... | collective-permute-start | bytes 1327112 | tf_op jit(solution)/shard_map/ppermute | solution.py:23
  131.1 1.9 collective-permute-done.5
  133.2 3.1 %collective-permute-start.6 = (bf16[96,1152]{1,0:T(8,128)(2,1)S(1)}, bf16[96,1152]{1,0:T(8,128)(2,1)S(1)}, u32[]{:S(2)}, u32[]{:S(2)}) collective-permute-start(bf16[96,1152]{1,0:T(8,128)(2,1)S(1)} %slice.88), channel_id=1, source_target_pairs={{0,96},{4,100},{8,104},{12,108},{16,112},{20,116},{24,120},{28,124... | collective-permute-start | bytes 663560 | tf_op jit(solution)/shard_map/ppermute | solution.py:23
  136.3 4.9 %collective-permute-done.1 = bf16[192,1152]{1,0:T(8,128)(2,1)S(1)} collective-permute-done((bf16[192,1152]{1,0:T(8,128)(2,1)S(1)}, bf16[192,1152]{1,0:T(8,128)(2,1)S(1)}, u32[]{:S(2)}, u32[]{:S(2)}) %collective-permute-start.1) | collective-permute-done | bytes 442400 | tf_op jit(solution)/shard_map/ppermute | solution.py:23
  142.9 2.6 %collective-permute-start.7 = (bf16[48,1152]{1,0:T(8,128)(2,1)S(1)}, bf16[48,1152]{1,0:T(8,128)(2,1)S(1)}, u32[]{:S(2)}, u32[]{:S(2)}) collective-permute-start(bf16[48,1152]{1,0:T(8,128)(2,1)S(1)} %slice.90), channel_id=1, source_target_pairs={{0,12},{4,8},{8,4},{12,0},{16,28},{20,24},{24,20},{28,16},{32,44},... | collective-permute-start | bytes 331784 | tf_op jit(solution)/shard_map/ppermute | solution.py:23
  149.6 2.6 %collective-permute-done.3 = bf16[48,1152]{1,0:T(8,128)(2,1)S(1)} collective-permute-done((bf16[48,1152]{1,0:T(8,128)(2,1)S(1)}, bf16[48,1152]{1,0:T(8,128)(2,1)S(1)}, u32[]{:S(2)}, u32[]{:S(2)}) %collective-permute-start.3) | collective-permute-done | bytes 110624 | tf_op jit(solution)/shard_map/ppermute | solution.py:23
  152.3 2.3 %collective-permute-start.4 = (bf16[24,1152]{1,0:T(8,128)(2,1)S(1)}, bf16[24,1152]{1,0:T(8,128)(2,1)S(1)}, u32[]{:S(2)}, u32[]{:S(2)}) collective-permute-start(bf16[24,1152]{1,0:T(8,128)(2,1)S(1)} %slice.93), channel_id=1, source_target_pairs={{0,96},{4,100},{8,104},{12,108},{16,112},{20,116},{24,120},{28,124... | collective-permute-start | bytes 165896 | tf_op jit(solution)/shard_map/ppermute | solution.py:23
  156.2 1.9 collective-permute-done.4.theirs_ref
  158.3 2.3 %collective-permute-start.10 = (bf16[24,1152]{1,0:T(8,128)(2,1)S(1)}, bf16[24,1152]{1,0:T(8,128)(2,1)S(1)}, u32[]{:S(2)}, u32[]{:S(2)}) collective-permute-start(bf16[24,1152]{1,0:T(8,128)(2,1)S(1)} %rescale.2), channel_id=1, source_target_pairs={{0,96},{4,100},{8,104},{12,108},{16,112},{20,116},{24,120},{28,124... | collective-permute-start | bytes 165896 | tf_op jit(solution)/shard_map/ppermute | solution.py:23
  160.6 2.5 %collective-permute-start.15 = (bf16[48,1152]{1,0:T(8,128)(2,1)S(1)}, bf16[48,1152]{1,0:T(8,128)(2,1)S(1)}, u32[]{:S(2)}, u32[]{:S(2)}) collective-permute-start(bf16[48,1152]{1,0:T(8,128)(2,1)S(1)} %pad_maximum_fusion.6), channel_id=1, source_target_pairs={{0,12},{4,8},{8,4},{12,0},{16,28},{20,24},{24,20},{28,16},{32,44},... | collective-permute-start | bytes 331784 | tf_op jit(solution)/shard_map/ppermute | solution.py:23
  163.8 2.8 %collective-permute-done.15 = bf16[48,1152]{1,0:T(8,128)(2,1)S(1)} collective-permute-done((bf16[48,1152]{1,0:T(8,128)(2,1)S(1)}, bf16[48,1152]{1,0:T(8,128)(2,1)S(1)}, u32[]{:S(2)}, u32[]{:S(2)}) %collective-permute-start.15) | collective-permute-done | bytes 110624 | tf_op jit(solution)/shard_map/ppermute | solution.py:23
  169.8 4.0 %collective-permute-done.16 = bf16[96,1152]{1,0:T(8,128)(2,1)S(1)} collective-permute-done((bf16[96,1152]{1,0:T(8,128)(2,1)S(1)}, bf16[96,1152]{1,0:T(8,128)(2,1)S(1)}, u32[]{:S(2)}, u32[]{:S(2)}) %collective-permute-start.16) | collective-permute-done | bytes 221216 | tf_op jit(solution)/shard_map/ppermute | solution.py:23
  174.6 2.5 %collective-permute-start.13 = (bf16[192,1152]{1,0:T(8,128)(2,1)S(1)}, bf16[192,1152]{1,0:T(8,128)(2,1)S(1)}, u32[]{:S(2)}, u32[]{:S(2)}) collective-permute-start(bf16[192,1152]{1,0:T(8,128)(2,1)S(1)} %pad_maximum_fusion.w_ref), channel_id=1, source_target_pairs={{0,12},{4,8},{8,4},{12,0},{16,28},{20,24},{24,20},{28,16},{32,44},... | collective-permute-start | bytes 1327112 | tf_op jit(solution)/shard_map/ppermute | solution.py:23
  178.8 9.9 %collective-permute-done.9.t1_ref = bf16[256,768]{1,0:T(8,128)(2,1)S(1)} collective-permute-done((bf16[256,768]{1,0:T(8,128)(2,1)S(1)}, bf16[256,768]{1,0:T(8,128)(2,1)S(1)}, u32[]{:S(2)}, u32[]{:S(2)}) %collective-permute-start.9) | collective-permute-done | bytes 393248 | tf_op jit(solution)/shard_map/ppermute | solution.py:23
  195.1 2.3 %collective-permute-done.19.r1_ref = bf16[256,384]{1,0:T(8,128)(2,1)S(1)} collective-permute-done((bf16[256,384]{1,0:T(8,128)(2,1)S(1)}, bf16[256,384]{1,0:T(8,128)(2,1)S(1)}, u32[]{:S(2)}, u32[]{:S(2)}) %collective-permute-start.19) | collective-permute-done | bytes 196640 | tf_op jit(solution)/shard_map/ppermute | solution.py:23
  197.4 2.1 %collective-permute-done.18.r0_ref = bf16[256,384]{1,0:T(8,128)(2,1)S(1)} collective-permute-done((bf16[256,384]{1,0:T(8,128)(2,1)S(1)}, bf16[256,384]{1,0:T(8,128)(2,1)S(1)}, u32[]{:S(2)}, u32[]{:S(2)}) %collective-permute-start.18) | collective-permute-done | bytes 196640 | tf_op jit(solution)/shard_map/ppermute | solution.py:23
  (99 shorter events, 37.7 us)
Async XLA Ops:
  0.6 76.4 %collective-permute-start = (bf16[512,768]{1,0:T(8,128)(2,1)}, bf16[512,768]{1,0:T(8,128)(2,1)}, u32[]{:S(2)}, u32[]{:S(2)}) collective-permute-start(bf16[512,768]{1,0:T(8,128)(2,1)} %t0_ref.2), channel_id=1, source_target_pairs={{0,4},{4,0},{8,12},{12,8},{16,20},{20,16},{24,28},{28,24},{32,36},... | collective-permute-start | bytes 2359304 | tf_op jit(solution)/shard_map/ppermute | solution.py:23
  11.8 55.8 %copy-start = (bf16[768,2304]{1,0:T(8,128)(2,1)S(1)}, bf16[768,2304]{1,0:T(8,128)(2,1)}, u32[]{:S(2)}) copy-start(bf16[768,2304]{1,0:T(8,128)(2,1)} %wv_ref.3) | copy-start | bytes 10616836
  84.3 24.9 %copy-start.3 = (bf16[512,768]{1,0:T(8,128)(2,1)S(1)}, bf16[512,768]{1,0:T(8,128)(2,1)}, u32[]{:S(2)}) copy-start(bf16[512,768]{1,0:T(8,128)(2,1)} %t0_ref.2) | copy-start | bytes 2359300
  84.3 24.9 %copy-start.4 = (bf16[768,1536]{1,0:T(8,128)(2,1)S(1)}, bf16[768,1536]{1,0:T(8,128)(2,1)}, u32[]{:S(2)}) copy-start(bf16[768,1536]{1,0:T(8,128)(2,1)} %wkv_ref.1) | copy-start | bytes 7077892
  121.1 11.9 %collective-permute-start.5 = (bf16[192,1152]{1,0:T(8,128)(2,1)S(1)}, bf16[192,1152]{1,0:T(8,128)(2,1)S(1)}, u32[]{:S(2)}, u32[]{:S(2)}) collective-permute-start(bf16[192,1152]{1,0:T(8,128)(2,1)S(1)} %gradient.7), channel_id=1, source_target_pairs={{0,32},{4,36},{8,40},{12,44},{16,48},{20,52},{24,56},{28,60},{32,0... | collective-permute-start | bytes 1327112 | tf_op jit(solution)/shard_map/ppermute | solution.py:23
  128.5 12.7 %collective-permute-start.1 = (bf16[192,1152]{1,0:T(8,128)(2,1)S(1)}, bf16[192,1152]{1,0:T(8,128)(2,1)S(1)}, u32[]{:S(2)}, u32[]{:S(2)}) collective-permute-start(bf16[192,1152]{1,0:T(8,128)(2,1)S(1)} %gradient.5), channel_id=1, source_target_pairs={{0,12},{4,8},{8,4},{12,0},{16,28},{20,24},{24,20},{28,16},{32,44},... | collective-permute-start | bytes 1327112 | tf_op jit(solution)/shard_map/ppermute | solution.py:23
  133.2 9.7 %collective-permute-start.6 = (bf16[96,1152]{1,0:T(8,128)(2,1)S(1)}, bf16[96,1152]{1,0:T(8,128)(2,1)S(1)}, u32[]{:S(2)}, u32[]{:S(2)}) collective-permute-start(bf16[96,1152]{1,0:T(8,128)(2,1)S(1)} %slice.88), channel_id=1, source_target_pairs={{0,96},{4,100},{8,104},{12,108},{16,112},{20,116},{24,120},{28,124... | collective-permute-start | bytes 663560 | tf_op jit(solution)/shard_map/ppermute | solution.py:23
  141.3 6.0 %collective-permute-start.2 = (bf16[96,1152]{1,0:T(8,128)(2,1)S(1)}, bf16[96,1152]{1,0:T(8,128)(2,1)S(1)}, u32[]{:S(2)}, u32[]{:S(2)}) collective-permute-start(bf16[96,1152]{1,0:T(8,128)(2,1)S(1)} %slice.89), channel_id=1, source_target_pairs={{0,16},{4,20},{8,24},{12,28},{16,0},{20,4},{24,8},{28,12},{32,48},... | collective-permute-start | bytes 663560 | tf_op jit(solution)/shard_map/ppermute | solution.py:23
  142.9 6.0 %collective-permute-start.7 = (bf16[48,1152]{1,0:T(8,128)(2,1)S(1)}, bf16[48,1152]{1,0:T(8,128)(2,1)S(1)}, u32[]{:S(2)}, u32[]{:S(2)}) collective-permute-start(bf16[48,1152]{1,0:T(8,128)(2,1)S(1)} %slice.90), channel_id=1, source_target_pairs={{0,12},{4,8},{8,4},{12,0},{16,28},{20,24},{24,20},{28,16},{32,44},... | collective-permute-start | bytes 331784 | tf_op jit(solution)/shard_map/ppermute | solution.py:23
  147.4 4.8 %collective-permute-start.3 = (bf16[48,1152]{1,0:T(8,128)(2,1)S(1)}, bf16[48,1152]{1,0:T(8,128)(2,1)S(1)}, u32[]{:S(2)}, u32[]{:S(2)}) collective-permute-start(bf16[48,1152]{1,0:T(8,128)(2,1)S(1)} %slice.91), channel_id=1, source_target_pairs={{0,32},{4,36},{8,40},{12,44},{16,48},{20,52},{24,56},{28,60},{32,0... | collective-permute-start | bytes 331784 | tf_op jit(solution)/shard_map/ppermute | solution.py:23
  149.0 5.5 %collective-permute-start.8 = (bf16[24,1152]{1,0:T(8,128)(2,1)S(1)}, bf16[24,1152]{1,0:T(8,128)(2,1)S(1)}, u32[]{:S(2)}, u32[]{:S(2)}) collective-permute-start(bf16[24,1152]{1,0:T(8,128)(2,1)S(1)} %slice.92), channel_id=1, source_target_pairs={{0,16},{4,20},{8,24},{12,28},{16,0},{20,4},{24,8},{28,12},{32,48},... | collective-permute-start | bytes 165896 | tf_op jit(solution)/shard_map/ppermute | solution.py:23
  152.3 5.9 %collective-permute-start.4 = (bf16[24,1152]{1,0:T(8,128)(2,1)S(1)}, bf16[24,1152]{1,0:T(8,128)(2,1)S(1)}, u32[]{:S(2)}, u32[]{:S(2)}) collective-permute-start(bf16[24,1152]{1,0:T(8,128)(2,1)S(1)} %slice.93), channel_id=1, source_target_pairs={{0,96},{4,100},{8,104},{12,108},{16,112},{20,116},{24,120},{28,124... | collective-permute-start | bytes 165896 | tf_op jit(solution)/shard_map/ppermute | solution.py:23
  154.6 5.9 %collective-permute-start.14 = (bf16[24,1152]{1,0:T(8,128)(2,1)S(1)}, bf16[24,1152]{1,0:T(8,128)(2,1)S(1)}, u32[]{:S(2)}, u32[]{:S(2)}) collective-permute-start(bf16[24,1152]{1,0:T(8,128)(2,1)S(1)} %rescale.3), channel_id=1, source_target_pairs={{0,16},{4,20},{8,24},{12,28},{16,0},{20,4},{24,8},{28,12},{32,48},... | collective-permute-start | bytes 165896 | tf_op jit(solution)/shard_map/ppermute | solution.py:23
  158.3 30.4 %copy-start.9 = (bf16[768,768]{1,0:T(8,128)(2,1)S(1)}, bf16[768,768]{1,0:T(8,128)(2,1)}, u32[]{:S(2)}) copy-start(bf16[768,768]{1,0:T(8,128)(2,1)} %w_ref.2) | copy-start | bytes 3538948
  158.3 5.4 %collective-permute-start.10 = (bf16[24,1152]{1,0:T(8,128)(2,1)S(1)}, bf16[24,1152]{1,0:T(8,128)(2,1)S(1)}, u32[]{:S(2)}, u32[]{:S(2)}) collective-permute-start(bf16[24,1152]{1,0:T(8,128)(2,1)S(1)} %rescale.2), channel_id=1, source_target_pairs={{0,96},{4,100},{8,104},{12,108},{16,112},{20,116},{24,120},{28,124... | collective-permute-start | bytes 165896 | tf_op jit(solution)/shard_map/ppermute | solution.py:23
  160.6 6.0 %collective-permute-start.15 = (bf16[48,1152]{1,0:T(8,128)(2,1)S(1)}, bf16[48,1152]{1,0:T(8,128)(2,1)S(1)}, u32[]{:S(2)}, u32[]{:S(2)}) collective-permute-start(bf16[48,1152]{1,0:T(8,128)(2,1)S(1)} %pad_maximum_fusion.6), channel_id=1, source_target_pairs={{0,12},{4,8},{8,4},{12,0},{16,28},{20,24},{24,20},{28,16},{32,44},... | collective-permute-start | bytes 331784 | tf_op jit(solution)/shard_map/ppermute | solution.py:23
  163.7 4.8 %collective-permute-start.11 = (bf16[48,1152]{1,0:T(8,128)(2,1)S(1)}, bf16[48,1152]{1,0:T(8,128)(2,1)S(1)}, u32[]{:S(2)}, u32[]{:S(2)}) collective-permute-start(bf16[48,1152]{1,0:T(8,128)(2,1)S(1)} %pad_maximum_fusion.5), channel_id=1, source_target_pairs={{0,32},{4,36},{8,40},{12,44},{16,48},{20,52},{24,56},{28,60},{32,0... | collective-permute-start | bytes 331784 | tf_op jit(solution)/shard_map/ppermute | solution.py:23
  166.6 7.2 %collective-permute-start.16 = (bf16[96,1152]{1,0:T(8,128)(2,1)S(1)}, bf16[96,1152]{1,0:T(8,128)(2,1)S(1)}, u32[]{:S(2)}, u32[]{:S(2)}) collective-permute-start(bf16[96,1152]{1,0:T(8,128)(2,1)S(1)} %pad_maximum_fusion.3), channel_id=1, source_target_pairs={{0,96},{4,100},{8,104},{12,108},{16,112},{20,116},{24,120},{28,124... | collective-permute-start | bytes 663560 | tf_op jit(solution)/shard_map/ppermute | solution.py:23
  168.6 6.0 %collective-permute-start.12 = (bf16[96,1152]{1,0:T(8,128)(2,1)S(1)}, bf16[96,1152]{1,0:T(8,128)(2,1)S(1)}, u32[]{:S(2)}, u32[]{:S(2)}) collective-permute-start(bf16[96,1152]{1,0:T(8,128)(2,1)S(1)} %pad_maximum_fusion.2), channel_id=1, source_target_pairs={{0,16},{4,20},{8,24},{12,28},{16,0},{20,4},{24,8},{28,12},{32,48},... | collective-permute-start | bytes 663560 | tf_op jit(solution)/shard_map/ppermute | solution.py:23
  173.9 17.1 %collective-permute-start.17 = (bf16[192,1152]{1,0:T(8,128)(2,1)S(1)}, bf16[192,1152]{1,0:T(8,128)(2,1)S(1)}, u32[]{:S(2)}, u32[]{:S(2)}) collective-permute-start(bf16[192,1152]{1,0:T(8,128)(2,1)S(1)} %pad_maximum_fusion.1.w_ref), channel_id=1, source_target_pairs={{0,32},{4,36},{8,40},{12,44},{16,48},{20,52},{24,56},{28,60},{32,0... | collective-permute-start | bytes 1327112 | tf_op jit(solution)/shard_map/ppermute | solution.py:23
  174.6 18.3 %collective-permute-start.13 = (bf16[192,1152]{1,0:T(8,128)(2,1)S(1)}, bf16[192,1152]{1,0:T(8,128)(2,1)S(1)}, u32[]{:S(2)}, u32[]{:S(2)}) collective-permute-start(bf16[192,1152]{1,0:T(8,128)(2,1)S(1)} %pad_maximum_fusion.w_ref), channel_id=1, source_target_pairs={{0,12},{4,8},{8,4},{12,0},{16,28},{20,24},{24,20},{28,16},{32,44},... | collective-permute-start | bytes 1327112 | tf_op jit(solution)/shard_map/ppermute | solution.py:23
  177.2 11.5 %collective-permute-start.9 = (bf16[256,768]{1,0:T(8,128)(2,1)S(1)}, bf16[256,768]{1,0:T(8,128)(2,1)S(1)}, u32[]{:S(2)}, u32[]{:S(2)}) collective-permute-start(bf16[256,768]{1,0:T(8,128)(2,1)S(1)} %copy-done.6), channel_id=1, source_target_pairs={{0,4},{4,0},{8,12},{12,8},{16,20},{20,16},{24,28},{28,24},{32,36},... | collective-permute-start | bytes 1179656 | tf_op jit(solution)/shard_map/ppermute | solution.py:23
  191.7 5.8 %collective-permute-start.19 = (bf16[256,384]{1,0:T(8,128)(2,1)S(1)}, bf16[256,384]{1,0:T(8,128)(2,1)S(1)}, u32[]{:S(2)}, u32[]{:S(2)}) collective-permute-start(bf16[256,384]{1,0:T(8,128)(2,1)S(1)} %get-tuple-element.32), channel_id=1, source_target_pairs={{0,4},{4,0},{8,12},{12,8},{16,20},{20,16},{24,28},{28,24},{32,36},... | collective-permute-start | bytes 589832 | tf_op jit(solution)/shard_map/ppermute | solution.py:23
  193.6 6.0 %collective-permute-start.18 = (bf16[256,384]{1,0:T(8,128)(2,1)S(1)}, bf16[256,384]{1,0:T(8,128)(2,1)S(1)}, u32[]{:S(2)}, u32[]{:S(2)}) collective-permute-start(bf16[256,384]{1,0:T(8,128)(2,1)S(1)} %get-tuple-element.31), channel_id=1, source_target_pairs={{0,4},{4,0},{8,12},{12,8},{16,20},{20,16},{24,28},{28,24},{32,36},... | collective-permute-start | bytes 589832 | tf_op jit(solution)/shard_map/ppermute | solution.py:23
  (10 other events, 119.0 us)

commit v2 on v1

v2 whole, which is shorter than its diff:
```python
import functools
import math

import jax
import jax.numpy as jnp
from jax import lax
from jax.experimental import pallas as pl
from jax.experimental.pallas import tpu as pltpu
from jax.sharding import PartitionSpec as P

eps = 1e-06
rate_base = 4.0
safe_temp = 60.0
bf16 = jnp.bfloat16
f32 = jnp.float32

pair_mask = 1
reduce_orders = ((3, 4, 8, 24), (24, 8, 3, 4))
split = 640


def swap(value, mask):
    pairs = [(source, source ^ mask) for source in range(lax.axis_size("tok"))]
    return lax.ppermute(value, "tok", pairs)


def params(mib):
    return pltpu.CompilerParams(vmem_limit_bytes=mib * 2**20)


def nn(a, b):
    return lax.dot_general(a, b, (((1,), (0,)), ((), ())), preferred_element_type=f32)


def nt(a, b):
    return lax.dot_general(a, b, (((1,), (1,)), ((), ())), preferred_element_type=f32)


def whole(shape):
    return pl.BlockSpec(shape, lambda *_: (0,) * len(shape))


smem = pl.BlockSpec(memory_space=pltpu.SMEM)


def gather_kernel(index_ref, rows_ref, out_ref):
    heads, blocks = index_ref.shape
    width = out_ref.shape[-1]
    for head in range(heads):
        for block in range(blocks):
            out_ref[head, block] = rows_ref[index_ref[head, block], :, head * width : head * width + width]


def gather_rows(index, rows):
    heads, blocks = index.shape
    _, height, width = rows.shape
    shape = (heads, blocks, height, width // heads)
    return pl.pallas_call(
        gather_kernel,
        grid=(1,),
        out_shape=jax.ShapeDtypeStruct(shape, rows.dtype),
        in_specs=[smem, whole(rows.shape)],
        out_specs=whole(shape),
        compiler_params=params(24),
        name="gather_rows",
    )(index, rows)


def qkv_kernel(valid_ref, tok_ref, gain_ref, scale_ref, wq_ref, wk_ref, wv_ref, q_ref, k_ref, v_ref, normed):
    @pl.when(pl.program_id(0) == 0)
    def _():
        x = tok_ref[...].astype(f32)
        unit = x * lax.rsqrt(jnp.mean(x * x, axis=-1, keepdims=True) + eps)
        normed[...] = (unit * gain_ref[...].astype(f32)).astype(bf16)

    rows = normed[...]
    count, cols = q_ref.shape[0], wq_ref.shape[1]
    low = lax.broadcasted_iota(jnp.int32, (count, 128), 1) < 64

    def unit_heads(t):
        square = t * t
        first = jnp.sum(jnp.where(low, square, 0.0), axis=-1, keepdims=True)
        second = jnp.sum(jnp.where(low, 0.0, square), axis=-1, keepdims=True)
        inv = [lax.rsqrt(total * (1.0 / 64.0) + eps) for total in (first, second)]
        return (t * jnp.where(low, inv[0], inv[1])).astype(bf16).astype(f32)

    query = nn(rows, wq_ref[...]).astype(bf16).astype(f32)
    key = nn(rows, wk_ref[...]).astype(bf16).astype(f32)
    value = nn(rows, wv_ref[...])
    live = lax.broadcasted_iota(jnp.int32, (count, 128), 0) < valid_ref[0]
    one = jnp.where(live, 1.0, 0.0)
    for tile in range(cols // 128):
        part = slice(tile * 128, tile * 128 + 128)
        even = slice(tile * 256, tile * 256 + 128)
        odd = slice(tile * 256 + 128, tile * 256 + 256)
        q = unit_heads(query[:, part]) * scale_ref[:, part]
        q_high = q.astype(bf16).astype(f32)
        moved = pltpu.roll(q - q_high, 64, 1)
        q_ref[:, even] = jnp.where(low, q_high, moved).astype(bf16)
        q_ref[:, odd] = jnp.where(low, moved, q_high).astype(bf16)
        k = unit_heads(key[:, part])
        moved = pltpu.roll(k, 64, 1)
        k_ref[:, even] = jnp.where(low, k, moved).astype(bf16)
        k_ref[:, odd] = jnp.where(low, moved, k).astype(bf16)
        shown = jnp.where(live, value[:, part], 0.0)
        v_ref[:, even] = jnp.where(low, shown, one).astype(bf16)
        v_ref[:, odd] = jnp.where(low, one, shown).astype(bf16)


def project_qkv(valid, tokens, gain, scale, weight):
    count, width = tokens.shape
    cols = 256
    steps = width // cols
    out = jax.ShapeDtypeStruct((count, 2 * width), bf16)
    return pl.pallas_call(
        qkv_kernel,
        grid=(steps,),
        out_shape=(out, out, out),
        in_specs=[
            smem,
            whole((count, width)),
            whole((1, width)),
            pl.BlockSpec((1, cols), lambda i: (0, i)),
            pl.BlockSpec((width, cols), lambda i: (0, i)),
            pl.BlockSpec((width, cols), lambda i: (0, steps + i)),
            pl.BlockSpec((width, cols), lambda i: (0, 2 * steps + i)),
        ],
        out_specs=[pl.BlockSpec((count, 2 * cols), lambda i: (0, i))] * 3,
        scratch_shapes=[pltpu.VMEM((count, width), bf16)],
        compiler_params=params(32),
        name="project_qkv",
    )(valid, tokens, gain, scale, weight, weight, weight)


def head_lanes(head):
    return slice(head * 128, head * 128 + 128)


def weighted(q, keys, values, lanes):
    total = None
    for k_ref, v_ref in zip(keys, values):
        part = nn(jnp.exp2(nt(q, k_ref[:, lanes])).astype(bf16), v_ref[:, lanes])
        total = part if total is None else total + part
    return total


def finish(sums, out_ref, start):
    count = sums[0].shape[0]
    low = lax.broadcasted_iota(jnp.int32, (count, 128), 1) < 64
    top = jnp.where(low, sums[0], sums[1])
    bottom = pltpu.roll(jnp.where(low, sums[1], sums[0]), 64, 1)
    out_ref[start : start + count, :] = (top / bottom).astype(bf16)


def is_plain(temp_ref):
    pair = pl.program_id(0)
    return jnp.maximum(temp_ref[2 * pair], temp_ref[2 * pair + 1]) <= safe_temp


def first_stage(temp_ref, q0, k0, v0, a0):
    @pl.when(is_plain(temp_ref))
    def _():
        for head in range(2):
            lanes = head_lanes(head)
            a0[:, lanes] = weighted(q0[:, lanes], [k0], [v0], lanes)


def second_stage(temp_ref, q0, k0, v0, q1, k1, v1, b0, a0, a1):
    @pl.when(is_plain(temp_ref))
    def _():
        for head in range(2):
            lanes = head_lanes(head)
            a0[:, lanes] = b0[:, lanes] + weighted(q0[:, lanes], [k1], [v1], lanes)
            a1[:, lanes] = weighted(q1[:, lanes], [k0, k1], [v0, v1], lanes)


def third_stage(valid_ref, temp_ref, q0, k0, v0, q1, k1, v1, q2, k2, v2, a0, a1, out_ref):
    starts = (0, q0.shape[0], q0.shape[0] + q1.shape[0])
    keys, values = [k0, k1, k2], [v0, v1, v2]

    @pl.when(is_plain(temp_ref))
    def _():
        for q_ref, a_ref, start in zip((q0, q1), (a0, a1), starts):
            finish(
                [
                    a_ref[:, head_lanes(head)] + weighted(q_ref[:, head_lanes(head)], [k2], [v2], head_lanes(head))
                    for head in range(2)
                ],
                out_ref,
                start,
            )
        finish([weighted(q2[:, head_lanes(head)], keys, values, head_lanes(head)) for head in range(2)], out_ref, starts[2])

    @pl.when(jnp.logical_not(is_plain(temp_ref)))
    def _():
        for q_ref, start in zip((q0, q1, q2), starts):
            for first in range(0, q_ref.shape[0], 256):
                sums = []
                for head in range(2):
                    lanes = head_lanes(head)
                    scores = []
                    for at, k_ref in enumerate(keys):
                        score = nt(q_ref[first : first + 256, lanes], k_ref[:, lanes])
                        spot = lax.broadcasted_iota(jnp.int32, score.shape, 1)
                        scores.append(jnp.where(spot < valid_ref[at], score, -1e30))
                    tops = [jnp.max(score, axis=-1, keepdims=True) for score in scores]
                    top = functools.reduce(jnp.maximum, tops)
                    total = 0.0
                    for score, v_ref in zip(scores, values):
                        total = total + nn(jnp.exp2(score - top).astype(bf16), v_ref[:, lanes])
                    sums.append(total)
                finish(sums, out_ref, start + first)


def columns(array):
    return pl.BlockSpec((array.shape[0], 256), lambda i: (0, i))


def stage(kernel, scalars, arrays, outs, name):
    return pl.pallas_call(
        kernel,
        grid=(arrays[0].shape[1] // 256,),
        out_shape=outs,
        in_specs=[smem] * len(scalars) + [columns(array) for array in arrays],
        out_specs=jax.tree.map(
            lambda out: pl.BlockSpec((out.shape[0], 256 * out.shape[1] // arrays[0].shape[1]), lambda i: (0, i)), outs
        ),
        compiler_params=params(40),
        name=name,
    )(*scalars, *arrays)


def push_rows(scale, live, after, wk_ref, wv_ref, r_ref, key_ref, push_ref):
    parts = nn(after, r_ref[...])
    high = parts[:, 0:1] + parts[:, 1:2] + parts[:, 2:3] + 1.0
    soft = jnp.maximum(high, 0.0) + jnp.log1p(jnp.exp(-jnp.abs(high)))
    spot = lax.broadcasted_iota(jnp.int32, high.shape, 0)
    rate = jnp.where(live(spot), soft * scale, 0.0)
    key = nn(after, wk_ref[...])
    key_ref[...] = (key * lax.rsqrt(jnp.mean(key * key, axis=-1, keepdims=True) + eps)).astype(bf16)
    push_ref[...] = (-rate * nn(after, wv_ref[...])).astype(bf16)


def shown_rows(valid_ref, side, count):
    return lambda spot: spot < valid_ref[side]


def out_kernel(scale, valid_ref, attn_ref, t0, t1, t2, wo_ref, wk_ref, wv_ref, r_ref, after_ref, key_ref, push_ref):
    side = pl.program_id(0)
    other = jnp.concatenate([t1[...], t2[...]], axis=0)
    before = jnp.where(side == 0, t0[...], other).astype(f32)
    after = (before + nn(attn_ref[...], wo_ref[...])).astype(bf16)
    after_ref[...] = after
    push_rows(scale, shown_rows(valid_ref, side, 0), after, wk_ref, wv_ref, r_ref, key_ref, push_ref)


def again_kernel(scale, valid_ref, after_ref, wk_ref, wv_ref, r_ref, key_ref, push_ref):
    side = pl.program_id(0)
    push_rows(scale, shown_rows(valid_ref, side, 0), after_ref[...], wk_ref, wv_ref, r_ref, key_ref, push_ref)


def head_weights(width, size, head):
    return [
        pl.BlockSpec((width, size), lambda i: (0, head)),
        pl.BlockSpec((width, size), lambda i: (0, width // size + head)),
        pl.BlockSpec((width, 128), lambda i: (0, head)),
    ]


def first_pushes(scale, valid, attn, t0, t1, t2, wo, wkv, rate):
    count, width = t0.shape
    size = width // (rate.shape[1] // 128)
    block = pl.BlockSpec((count, width), lambda i: (i, 0))
    narrow = pl.BlockSpec((count, size), lambda i: (i, 0))
    both = jax.ShapeDtypeStruct((2 * count, size), bf16)
    return pl.pallas_call(
        functools.partial(out_kernel, scale),
        grid=(2,),
        out_shape=(jax.ShapeDtypeStruct((2 * count, width), bf16), both, both),
        in_specs=[smem, block] + [whole(t.shape) for t in (t0, t1, t2, wo)] + head_weights(width, size, 0),
        out_specs=[block, narrow, narrow],
        compiler_params=params(32),
        name="first_pushes",
    )(valid, attn, t0, t1, t2, wo, wkv, wkv, rate)


def next_pushes(scale, valid, after, wkv, rate, head):
    rows, width = after.shape
    count = rows // 2
    size = width // (rate.shape[1] // 128)
    narrow = pl.BlockSpec((count, size), lambda i: (i, 0))
    both = jax.ShapeDtypeStruct((rows, size), bf16)
    return pl.pallas_call(
        functools.partial(again_kernel, scale),
        grid=(2,),
        out_shape=(both, both),
        in_specs=[smem, pl.BlockSpec((count, width), lambda i: (i, 0))] + head_weights(width, size, head),
        out_specs=[narrow, narrow],
        compiler_params=params(32),
        name="next_pushes",
    )(valid, after, wkv, wkv, rate)


def grad_rows(w, key, push):
    size = key.shape[1]
    act_a = nt(w[:, :size], key)
    act_b = nt(w[:, size : 2 * size], key)
    back = nt(w[:, 2 * size :], push)
    sigma = 1.0 / (1.0 + jnp.exp(-act_a))
    silu = act_a * sigma
    hidden = (silu * act_b).astype(bf16)
    grad_a = (back * act_b * sigma * (1.0 + act_a * (1.0 - sigma))).astype(bf16)
    grad_b = (back * silu).astype(bf16)
    return nn(grad_a, key), nn(grad_b, key), nn(hidden, push)


def sent_kernel(w_ref, key_ref, push_ref, first_ref, second_ref, first_keep, second_keep):
    quarter = first_keep.shape[0]
    size = key_ref.shape[1]
    rest = split - size
    a, b, c = grad_rows(w_ref[0, quarter:, :], key_ref[...], push_ref[...])
    early, middle, late = slice(0, quarter), slice(quarter, 2 * quarter), slice(2 * quarter, 3 * quarter)
    first_ref[:, :size] = a[quarter:].astype(bf16)
    first_ref[:, size:] = b[quarter:, :rest].astype(bf16)
    first_keep[:, :size] = a[early]
    first_keep[:, size:] = b[early, :rest]
    second_ref[:quarter, : size - rest] = b[early, rest:].astype(bf16)
    second_ref[:quarter, size - rest :] = c[early].astype(bf16)
    second_ref[quarter:, : size - rest] = b[late, rest:].astype(bf16)
    second_ref[quarter:, size - rest :] = c[late].astype(bf16)
    second_keep[:, : size - rest] = b[middle, rest:]
    second_keep[:, size - rest :] = c[middle]


def sent_gradient(weights, keys, pushes, head):
    _, rows, cols = weights.shape
    quarter = rows // 4
    shapes = [(2 * quarter, split), (2 * quarter, cols - split), (quarter, split), (quarter, cols - split)]
    kinds = [bf16, bf16, f32, f32]
    return pl.pallas_call(
        sent_kernel,
        grid=(1,),
        out_shape=tuple(jax.ShapeDtypeStruct(shape, kind) for shape, kind in zip(shapes, kinds)),
        in_specs=[pl.BlockSpec((1, rows, cols), lambda i: (head, 0, 0)), whole(keys.shape), whole(pushes.shape)],
        out_specs=[whole(shape) for shape in shapes],
        compiler_params=params(32),
        name="sent_gradient",
    )(weights, keys, pushes)


def kept_kernel(w_ref, key_ref, push_ref, out_ref):
    size = key_ref.shape[1]
    for at, part in enumerate(grad_rows(w_ref[0], key_ref[...], push_ref[...])):
        out_ref[:, at * size : at * size + size] = part


def kept_gradient(weights, keys, pushes, head):
    _, rows, cols = weights.shape
    quarter = rows // 4
    return pl.pallas_call(
        kept_kernel,
        grid=(1,),
        out_shape=jax.ShapeDtypeStruct((quarter, cols), f32),
        in_specs=[pl.BlockSpec((1, quarter, cols), lambda i: (head, 0, 0)), whole(keys.shape), whole(pushes.shape)],
        out_specs=whole((quarter, cols)),
        compiler_params=params(32),
        name="kept_gradient",
    )(weights, keys, pushes)


def join_kernel(kept_ref, a1_ref, b1_ref, a2_ref, b2_ref, sent_ref, keep_ref):
    half = keep_ref.shape[0]
    quarter = kept_ref.shape[0]
    for first, second, part in ((a1_ref, a2_ref, slice(0, split)), (b1_ref, b2_ref, slice(split, kept_ref.shape[1]))):
        total = kept_ref[:, part] + first[:quarter, :].astype(f32) + second[...].astype(f32)
        keep_ref[:, part] = total[:half]
        sent_ref[:, part] = total[half:].astype(bf16)


def join(kept, *got):
    half = (kept.shape[0] // 2, kept.shape[1])
    return pl.pallas_call(
        join_kernel,
        grid=(1,),
        out_shape=(jax.ShapeDtypeStruct(half, bf16), jax.ShapeDtypeStruct(half, f32)),
        in_specs=[whole(kept.shape)] + [whole(part.shape) for part in got],
        out_specs=[whole(half)] * 2,
        compiler_params=params(8),
        name="join",
    )(kept, *got)


def rescale_kernel(start_ref, mine_ref, theirs_ref, out_ref):
    size = start_ref.shape[1] // 3
    grad = mine_ref[...] + theirs_ref[...].astype(f32)
    for block in range(3):
        part = slice(block * size, block * size + size)
        start = start_ref[:, part].astype(f32)
        update = start - grad[:, part]
        before = jnp.sqrt(jnp.mean(start * start, axis=-1, keepdims=True) + eps)
        after = lax.rsqrt(jnp.mean(update * update, axis=-1, keepdims=True) + eps)
        out_ref[:, part] = (update * before * after).astype(bf16)


def rescale(start, mine, theirs):
    return pl.pallas_call(
        rescale_kernel,
        grid=(1,),
        out_shape=jax.ShapeDtypeStruct(start.shape, bf16),
        in_specs=[whole(start.shape)] * 3,
        out_specs=whole(start.shape),
        compiler_params=params(8),
        name="rescale",
    )(start, mine, theirs)


def query_kernel(t0_ref, t1_ref, w_ref, out_ref):
    side = pl.program_id(0)
    width = t0_ref.shape[1]
    size = width // 2
    tq = nn(jnp.where(side == 0, t0_ref[...], t1_ref[...]), w_ref[...])
    for head in range(2):
        part = slice(head * size, head * size + size)
        q = tq[:, part]
        out_ref[:, part] = (q * lax.rsqrt(jnp.mean(q * q, axis=-1, keepdims=True) + eps)).astype(bf16)


def target_queries(t0, t1, weight):
    count, width = t0.shape
    return pl.pallas_call(
        query_kernel,
        grid=(2,),
        out_shape=jax.ShapeDtypeStruct((2 * count, width), bf16),
        in_specs=[whole((count, width))] * 2 + [whole(weight.shape)],
        out_specs=pl.BlockSpec((count, width), lambda i: (i, 0)),
        compiler_params=params(16),
        name="target_queries",
    )(t0, t1, weight)


def apply_kernel(q_ref, h_ref, a3, b3, a4, b4, mine_ref, theirs_ref):
    count = mine_ref.shape[0]
    size = q_ref.shape[1]
    rest = split - size
    quarter = h_ref.shape[0]
    q = q_ref[...]
    total = 0.0
    blocks = (
        (h_ref[:, :split], h_ref[:, split:]),
        (a3[...], b4[:quarter, :]),
        (a4[:quarter, :], b3[...]),
        (a4[quarter:, :], b4[quarter:, :]),
    )
    for first, second in blocks:
        act_a = nt(q, first[:, :size])
        act_b = nt(q[:, :rest], first[:, size:]) + nt(q[:, rest:], second[:, : size - rest])
        hidden = (act_a / (1.0 + jnp.exp(-act_a)) * act_b).astype(bf16)
        total = total + nn(hidden, second[:, size - rest :])
    mine_ref[...] = total[:count]
    theirs_ref[...] = total[count:].astype(bf16)


def apply_weights(queries, parts, head):
    count = queries.shape[0]
    size = (parts[0].shape[1]) // 3
    half = (count // 2, size)
    return pl.pallas_call(
        apply_kernel,
        grid=(1,),
        out_shape=(jax.ShapeDtypeStruct(half, f32), jax.ShapeDtypeStruct(half, bf16)),
        in_specs=[pl.BlockSpec((count, size), lambda i: (0, head))] + [whole(part.shape) for part in parts],
        out_specs=[whole(half)] * 2,
        compiler_params=params(16),
        name="apply_weights",
    )(queries, *parts)


def merge_kernel(used_ref, target_ref, w_ref, m0_ref, m1_ref, r0_ref, r1_ref, out_ref):
    size = m0_ref.shape[1]
    total = target_ref[...].astype(f32)
    for head, (mine, theirs) in enumerate(((m0_ref, r0_ref), (m1_ref, r1_ref))):
        fout = mine[...] + theirs[...].astype(f32)
        unit = (fout * lax.rsqrt(jnp.mean(fout * fout, axis=-1, keepdims=True) + eps)).astype(bf16)
        total = total + nn(unit, w_ref[head * size : head * size + size, :])
    live = lax.broadcasted_iota(jnp.int32, total.shape, 0) < used_ref[0]
    out_ref[...] = jnp.where(live, total, 0.0).astype(bf16)


def merge(used, target, weight, mine, theirs):
    return pl.pallas_call(
        merge_kernel,
        grid=(1,),
        out_shape=jax.ShapeDtypeStruct(target.shape, bf16),
        in_specs=[smem, whole(target.shape), whole(weight.shape)] + [whole(mine[0].shape)] * 4,
        out_specs=whole(target.shape),
        compiler_params=params(16),
        name="merge",
    )(used, target, weight, *mine, *theirs)


def split_weight(value):
    parts = []
    for _ in range(3):
        part = lax.reduce_precision(value, 8, 7)
        parts.append(part.astype(bf16))
        value = value - part
    return parts


def body(
    tokens,
    attn_gain,
    qkv_weight,
    head_temp,
    out_weight,
    kv_weight,
    rate_weight,
    fast_weights,
    target,
    query_weight,
    merge_weight,
    image_lengths,
    target_counts,
):
    tok_rows, width = tokens.shape
    devices = lax.axis_size("tok")
    place = lax.axis_index("tok")
    parity = place % 2
    head_dim = width // head_temp.shape[0]
    fast_hidden, fast_cols = fast_weights.shape
    fast_heads = rate_weight.shape[1]
    rows = fast_hidden // devices
    image_ids = jnp.arange(image_lengths.shape[0], dtype=jnp.int32)
    length = jnp.sum(jnp.where(image_ids == place // 2, image_lengths, 0))
    own = length - parity * tok_rows
    other = length - (1 - parity) * tok_rows
    chunk = tok_rows // 2
    valid = jnp.stack([own, other, other - chunk]).astype(jnp.int32)

    t1 = swap(tokens[:chunk], pair_mask)

    scale = jnp.repeat(head_temp * (math.log2(math.e) / head_dim), head_dim)[None, :]
    gain = attn_gain[None, :]
    q0, k0, v0 = project_qkv(valid[:1], tokens, gain, scale, qkv_weight)
    late, q0 = lax.optimization_barrier((tokens[chunk:], q0))
    t2 = swap(late, pair_mask)

    moves = []
    for order in reduce_orders:
        span = [0]
        for mask in reversed(order):
            span = span + [mask ^ at for at in span]
        moves.append(span)
    index = place ^ jnp.array(moves, dtype=jnp.int32)
    start = gather_rows(index, fast_weights.reshape(devices, rows, fast_cols))
    weights = start.reshape(fast_heads, len(moves[0]) * rows, fast_cols // fast_heads)
    rate = jnp.stack(split_weight(rate_weight), axis=-1)
    rate = jnp.pad(rate, ((0, 0), (0, 0), (0, 125))).reshape(width, fast_heads * 128)

    wide = 2 * width
    sums0 = jax.ShapeDtypeStruct((tok_rows, wide), f32)
    sums1 = jax.ShapeDtypeStruct((chunk, wide), f32)
    a0 = stage(first_stage, [head_temp], [q0, k0, v0], sums0, "attend_first")
    q1, k1, v1 = project_qkv(valid[1:2], t1, gain, scale, qkv_weight)
    a0, a1 = stage(
        second_stage, [head_temp], [q0, k0, v0, q1, k1, v1, a0], (sums0, sums1), "attend_second"
    )
    t2, target_sent = lax.optimization_barrier((t2, target))
    other_target = swap(target_sent, pair_mask)
    q2, k2, v2 = project_qkv(valid[2:], t2, gain, scale, qkv_weight)
    attn = stage(
        third_stage,
        [valid, head_temp],
        [q0, k0, v0, q1, k1, v1, q2, k2, v2, a0, a1],
        jax.ShapeDtypeStruct((2 * tok_rows, width), bf16),
        "attend_third",
    )

    factor = rate_base / (tok_rows * devices)
    after, keys, pushes = first_pushes(factor, valid, attn, tokens, t1, t2, out_weight, kv_weight, rate)
    made = [(keys, pushes)]
    sent = [sent_gradient(weights, keys, pushes, 0)]
    after, other_target = lax.optimization_barrier((after, other_target))
    for head in range(1, fast_heads):
        made.append(next_pushes(factor, valid, after, kv_weight, rate, head))
        sent.append(sent_gradient(weights, *made[head], head))
    kept = [kept_gradient(weights, *made[head], head) for head in range(fast_heads)]

    fresh = []
    for head in range(fast_heads):
        d1, d2, d3, d4 = reduce_orders[head]
        first, second, first_keep, second_keep = sent[head]
        quarter = first_keep.shape[0]
        a1, b1 = swap(first, d1), swap(second, d2)
        a2 = swap((first_keep + a1[quarter:].astype(f32)).astype(bf16), d2)
        b2 = swap((second_keep + b1[quarter:].astype(f32)).astype(bf16), d1)
        away, stay = join(kept[head], a1, b1, a2, b2)
        total = stay + swap(away, d3).astype(f32)
        got = swap(total[rows:].astype(bf16), d4)
        fresh.append(rescale(start[head, 0], total[:rows], got))

    queries = target_queries(target, other_target, query_weight)
    mine, theirs = [], []
    for head in range(fast_heads):
        d1, d2, d3, d4 = reduce_orders[head]
        held = fresh[head]
        for mask in (d4, d3):
            held = jnp.concatenate([held, swap(held, mask)], axis=0)
        first, second = held[:, :split], held[:, split:]
        a3, b3 = swap(first, d2), swap(second, d1)
        a4 = swap(jnp.concatenate([first, a3], axis=0), d1)
        b4 = swap(jnp.concatenate([second, b3], axis=0), d2)
        kept_sum, sent_sum = apply_weights(queries, [held, a3, b3, a4, b4], head)
        mine.append(kept_sum)
        theirs.append(swap(sent_sum, pair_mask))
    target_out = merge(target_counts, target, merge_weight, mine, theirs)
    return (after[:tok_rows], jnp.concatenate(fresh, axis=1), target_out)


def solution(mesh):
    placed = (
        P(("rep", "tok"), None),
        P(),
        P(),
        P(),
        P(),
        P(),
        P(),
        P(),
        P(("rep", "tok"), None),
        P(),
        P(),
        P("rep"),
        P(("rep", "tok")),
    )
    return jax.shard_map(
        body,
        mesh=mesh,
        in_specs=placed,
        out_specs=(P(("rep", "tok"), None), P(("rep", "tok"), None), P(("rep", "tok"), None)),
        check_vma=False,
    )
```

time: 202 us -> 154 us (0.76)
  Pallas kernels: 117 us -> 65.9 us
  waiting for transfers between devices: 37.4 us -> 30.6 us
  starting transfers between devices: 31.8 us -> 38 us
  local copies, waits for them, and re-layouts: 7.88 us -> 13.5 us
  other arithmetic: 4.36 us -> 2.31 us
    pallas_call x11 -> x14, Pallas kernels: 100 us -> 50.1 us  [the longest x3 30.1 us: stage(): pl.pallas_call(kernel, grid=(arrays[0].shape[1] // 256,), out_shape=outs,...]
    unnamed x29 -> x40, local copies, waits for them, and re-layouts: 2.01 us -> 9.85 us
    ppermute x20 -> x29, waiting for transfers between devices: 37.4 us -> 30.6 us  [swap(): return lax.ppermute(value, 'tok', pairs)]
    ppermute x20 -> x29, starting transfers between devices: 31.8 us -> 38 us  [swap(): return lax.ppermute(value, 'tok', pairs)]
    slice x8 -> x10, local copies, waits for them, and re-layouts: 0.12 us -> 3.06 us  [the longest x1 2.06 us: body(): t1 = swap(tokens[:chunk], pair_mask)]
    broadcast_in_dim x3 -> x0, local copies, waits for them, and re-layouts: 2.92 us -> none  [body(): jnp.broadcast_to(part[:, :, None], part.shape + (128,))]
    pallas_call x2 -> x3, Pallas kernels: 13.4 us -> 13 us  [project_qkv(): pl.pallas_call(qkv_kernel, grid=(steps,), out_shape=(out, out, out), in_s...]
  transfers between devices with their start and end apart: 20 -> 29, of which waited for: 14 -> 18; matrix products, arithmetic and copies ran while one was open for 5% -> 3% of each run, Pallas kernels for 35% -> 16%
where the time goes in v2:
time: 154 us; the launch traced here: 153 us
  Pallas kernels  65.9 us (43%)
  starting transfers between devices  38 us (25%)
  waiting for transfers between devices  30.6 us (20%)
  local copies, waits for them, and re-layouts  13.5 us (9%)
  between operations  3.06 us (2%)
  other arithmetic  2.31 us (2%)
    ppermute x29, starting transfers between devices, swap(): return lax.ppermute(value, 'tok', pairs)  38 us
    ppermute x29, waiting for transfers between devices, swap(): return lax.ppermute(value, 'tok', pairs)  30.6 us
    pallas_call x3, Pallas kernels, stage(): pl.pallas_call(kernel, grid=(arrays[0].shape[1] // 256,), out_shape=outs,...  30.1 us
    pallas_call x3, Pallas kernels, project_qkv(): pl.pallas_call(qkv_kernel, grid=(steps,), out_shape=(out, out, out), in_s...  13 us
    unnamed x40, local copies, waits for them, and re-layouts  9.85 us
    pallas_call x1, Pallas kernels, first_pushes(): pl.pallas_call(functools.partial(out_kernel, scale), grid=(2,), out_shape...  5.34 us
    pallas_call x2, Pallas kernels, sent_gradient(): pl.pallas_call(sent_kernel, grid=(1,), out_shape=tuple((jax.ShapeDtypeStr...  4.62 us
    pallas_call x2, Pallas kernels, apply_weights(): pl.pallas_call(apply_kernel, grid=(1,), out_shape=(jax.ShapeDtypeStruct(h...  3.36 us
  transfers between devices with their start and end apart: 29, of which 18 were waited for; matrix products, arithmetic and copies ran while one was open for 3% of the time, Pallas kernels for 16%

profile of v2, /device:TPU:0, one launch (start us, length us, event | category | flops | bytes accessed | tf_op | source)
XLA Modules:
  0.0 153.4 jit_solution(11467953062715471157)
XLA Ops:
  0.7 2.1 %fusion.6 = (bf16[256,768]{1,0:T(8,128)(2,1)}, bf16[256,768]{1,0:T(8,128)(2,1)}) fusion(bf16[512,768]{1,0:T(8,128)(2,1)} %t0.1), kind=kLoop, calls=%fused_computation.35 | loop fusion | bytes 1572864 | tf_op jit(solution)/shard_map/slice | solution.py:540
  9.4 5.1 %project_qkv.3 = (bf16[512,1536]{1,0:T(8,128)(2,1)S(1)}, bf16[512,1536]{1,0:T(8,128)(2,1)S(1)}, bf16[512,1536]{1,0:T(8,128)(2,1)S(1)}) custom-call(s32[1]{0:T(128)} %bitcast.valid_ref, bf16[512,768]{1,0:T(8,128)(2,1)S(1)} %copy-done.6, bf16[1,768]{1,0:T(2,128)(2,1)S(1)} %broadcast_in_dim.11.gain_ref, f32[1,768]{1,0:T(1,128)S(1)} %broadcast_in_dim_reshape.3.scale_ref, ...), custom_call_target="tpu_custom_call" | custom-call | tf_op jit(solution)/shard_map/project_qkv/pallas_call | solution.py:115
  22.0 2.1 %attend_first.1.b0 = f32[512,1536]{1,0:T(8,128)S(1)} custom-call(f32[12]{0:T(128)S(1)} %copy-done.14, bf16[512,1536]{1,0:T(8,128)(2,1)S(1)} %get-tuple-element.42.q0, bf16[512,1536]{1,0:T(8,128)(2,1)S(1)} %get-tuple-element.43.k0, bf16[512,1536]{1,0:T(8,128)(2,1)S(1)} %copy-done.4), custom_call_target="tpu_custom_call" | custom-call | tf_op jit(solution)/shard_map/attend_first/pallas_call | solution.py:220
  24.2 2.4 %collective-permute-done.1.tok_ref.t2 = bf16[256,768]{1,0:T(8,128)(2,1)} collective-permute-done((bf16[256,768]{1,0:T(8,128)(2,1)}, bf16[256,768]{1,0:T(8,128)(2,1)}, u32[]{:S(2)}, u32[]{:S(2)}) %collective-permute-start.1) | collective-permute-done | bytes 393248 | tf_op jit(solution)/shard_map/ppermute | solution.py:24
  26.6 3.9 %project_qkv.5 = (bf16[256,1536]{1,0:T(8,128)(2,1)S(1)}, bf16[256,1536]{1,0:T(8,128)(2,1)S(1)}, bf16[256,1536]{1,0:T(8,128)(2,1)S(1)}) custom-call(s32[1]{0:T(128)} %bitcast.2.valid_ref, bf16[256,768]{1,0:T(8,128)(2,1)} %collective-permute-done.1.tok_ref.t2, bf16[1,768]{1,0:T(2,128)(2,1)S(1)} %broadcast_in_dim.11.gain_ref, ...), custom_call_target="tpu_custom_call" | custom-call | tf_op jit(solution)/shard_map/project_qkv/pallas_call | solution.py:115
  30.5 4.0 %project_qkv.4 = (bf16[256,1536]{1,0:T(8,128)(2,1)S(1)}, bf16[256,1536]{1,0:T(8,128)(2,1)S(1)}, bf16[256,1536]{1,0:T(8,128)(2,1)S(1)}) custom-call(s32[1]{0:T(128)} %bitcast.1.valid_ref, bf16[256,768]{1,0:T(8,128)(2,1)} %collective-permute-done.tok_ref.t1, bf16[1,768]{1,0:T(2,128)(2,1)S(1)} %broadcast_in_dim.11.gain_ref, ...), custom_call_target="tpu_custom_call" | custom-call | tf_op jit(solution)/shard_map/project_qkv/pallas_call | solution.py:115
  34.5 4.9 %attend_second.1 = (f32[512,1536]{1,0:T(8,128)S(1)}, f32[256,1536]{1,0:T(8,128)S(1)}) custom-call(f32[12]{0:T(128)S(1)} %copy-done.14, bf16[512,1536]{1,0:T(8,128)(2,1)S(1)} %get-tuple-element.42.q0, bf16[512,1536]{1,0:T(8,128)(2,1)S(1)} %get-tuple-element.43.k0, bf16[512,1536]{1,0:T(8,128)(2,1)S(1)} %copy-done.4, ...), custom_call_target="tpu_custom_call" | custom-call | tf_op jit(solution)/shard_map/attend_second/pallas_call | solution.py:220
  41.0 23.2 %attend_third.1.attn_ref = bf16[1024,768]{1,0:T(8,128)(2,1)S(1)} custom-call(s32[3]{0:T(128)S(1)} %pad_add_fusion.valid_ref, f32[12]{0:T(128)S(1)} %copy-done.14, bf16[512,1536]{1,0:T(8,128)(2,1)S(1)} %get-tuple-element.42.q0, bf16[512,1536]{1,0:T(8,128)(2,1)S(1)} %get-tuple-element.43.k0, bf16[512,1536]{1,0:T(8,128)(2,1)S(1)} %copy-done.4, ...), custom_call_target="tpu_custom_call" | custom-call | tf_op jit(solution)/shard_map/attend_third/pallas_call | solution.py:220
  64.2 5.3 %first_pushes.1 = (bf16[1024,768]{1,0:T(8,128)(2,1)S(1)}, bf16[1024,384]{1,0:T(8,128)(2,1)S(1)}, bf16[1024,384]{1,0:T(8,128)(2,1)S(1)}) custom-call(s32[3]{0:T(128)S(1)} %pad_add_fusion.valid_ref, bf16[1024,768]{1,0:T(8,128)(2,1)S(1)} %attend_third.1.attn_ref, bf16[512,768]{1,0:T(8,128)(2,1)S(1)} %copy-done.7, ...), custom_call_target="tpu_custom_call" | custom-call | tf_op jit(solution)/shard_map/first_pushes/pallas_call | solution.py:276
  69.6 2.4 %sent_gradient.2 = (bf16[192,640]{1,0:T(8,128)(2,1)S(1)}, bf16[192,512]{1,0:T(8,128)(2,1)S(1)}, f32[96,640]{1,0:T(8,128)S(1)}, f32[96,512]{1,0:T(8,128)S(1)}) custom-call(bf16[2,384,1152]{2,1,0:T(8,128)(2,1)S(1)} %bitcast.19, bf16[1024,384]{1,0:T(8,128)(2,1)S(1)} %get-tuple-element.58.key_ref, bf16[1024,384]{1,0:T(8,128)(2,1)S(1)} %get-tuple-element.59.push_ref), custom_call_target="tpu_custom_call" | custom-call | tf_op jit(solution)/shard_map/sent_gradient/pallas_call | solution.py:340
  72.0 2.6 %collective-permute-start.3 = (bf16[192,640]{1,0:T(8,128)(2,1)S(1)}, bf16[192,640]{1,0:T(8,128)(2,1)S(1)}, u32[]{:S(2)}, u32[]{:S(2)}) collective-permute-start(bf16[192,640]{1,0:T(8,128)(2,1)S(1)} %get-tuple-element.60), channel_id=1, source_target_pairs={{0,12},{4,8},{8,4},{12,0},{16,28},{20,24},{24,20},{28,16},{32,44},... | collective-permute-start | bytes 737288 | tf_op jit(solution)/shard_map/ppermute | solution.py:24
  77.1 2.7 %collective-permute-done.3.a1_ref = bf16[192,640]{1,0:T(8,128)(2,1)S(1)} collective-permute-done((bf16[192,640]{1,0:T(8,128)(2,1)S(1)}, bf16[192,640]{1,0:T(8,128)(2,1)S(1)}, u32[]{:S(2)}, u32[]{:S(2)}) %collective-permute-start.3) | collective-permute-done | bytes 245792 | tf_op jit(solution)/shard_map/ppermute | solution.py:24
  81.4 2.9 %collective-permute-done.2.t1_ref = bf16[256,768]{1,0:T(8,128)(2,1)S(1)} collective-permute-done((bf16[256,768]{1,0:T(8,128)(2,1)S(1)}, bf16[256,768]{1,0:T(8,128)(2,1)S(1)}, u32[]{:S(2)}, u32[]{:S(2)}) %collective-permute-start.2) | collective-permute-done | bytes 393248 | tf_op jit(solution)/shard_map/ppermute | solution.py:24
  84.3 3.0 %next_pushes.1 = (bf16[1024,384]{1,0:T(8,128)(2,1)S(1)}, bf16[1024,384]{1,0:T(8,128)(2,1)S(1)}) custom-call(s32[3]{0:T(128)S(1)} %pad_add_fusion.valid_ref, bf16[1024,768]{1,0:T(8,128)(2,1)S(1)} %get-tuple-element.57.after_ref, bf16[768,1536]{1,0:T(8,128)(2,1)S(1)} %copy-done.2, bf16[768,1536]{1,0:T(8,128)(2,1)S(1)} %copy-done.2, bf16[768,256]{1,0:T(8,128)(2,1)S(1)} %bitcast.24), custom_call_target="tpu_custom_call" | custom-call | tf_op jit(solution)/shard_map/next_pushes/pallas_call | solution.py:293
  87.2 2.3 %sent_gradient.3 = (bf16[192,640]{1,0:T(8,128)(2,1)S(1)}, bf16[192,512]{1,0:T(8,128)(2,1)S(1)}, f32[96,640]{1,0:T(8,128)S(1)}, f32[96,512]{1,0:T(8,128)S(1)}) custom-call(bf16[2,384,1152]{2,1,0:T(8,128)(2,1)S(1)} %bitcast.20, bf16[1024,384]{1,0:T(8,128)(2,1)S(1)} %get-tuple-element.66.key_ref, bf16[1024,384]{1,0:T(8,128)(2,1)S(1)} %get-tuple-element.67.push_ref), custom_call_target="tpu_custom_call" | custom-call | tf_op jit(solution)/shard_map/sent_gradient/pallas_call | solution.py:340
  91.7 2.2 %collective-permute-start.9 = (bf16[192,640]{1,0:T(8,128)(2,1)S(1)}, bf16[192,640]{1,0:T(8,128)(2,1)S(1)}, u32[]{:S(2)}, u32[]{:S(2)}) collective-permute-start(bf16[192,640]{1,0:T(8,128)(2,1)S(1)} %get-tuple-element.68), channel_id=1, source_target_pairs={{0,96},{4,100},{8,104},{12,108},{16,112},{20,116},{24,120},{28,124... | collective-permute-start | bytes 737288 | tf_op jit(solution)/shard_map/ppermute | solution.py:24
  97.7 3.1 %collective-permute-start.12 = (bf16[96,512]{1,0:T(8,128)(2,1)S(1)}, bf16[96,512]{1,0:T(8,128)(2,1)S(1)}, u32[]{:S(2)}, u32[]{:S(2)}) collective-permute-start(bf16[96,512]{1,0:T(8,128)(2,1)S(1)} %add_convert_fusion.2), channel_id=1, source_target_pairs={{0,96},{4,100},{8,104},{12,108},{16,112},{20,116},{24,120},{28,124... | collective-permute-start | bytes 294920 | tf_op jit(solution)/shard_map/ppermute | solution.py:24
  103.7 2.2 %collective-permute-done.11.a2_ref = bf16[96,640]{1,0:T(8,128)(2,1)S(1)} collective-permute-done((bf16[96,640]{1,0:T(8,128)(2,1)S(1)}, bf16[96,640]{1,0:T(8,128)(2,1)S(1)}, u32[]{:S(2)}, u32[]{:S(2)}) %collective-permute-start.11) | collective-permute-done | bytes 122912 | tf_op jit(solution)/shard_map/ppermute | solution.py:24
  105.9 2.2 %collective-permute-start.13 = (bf16[48,1152]{1,0:T(8,128)(2,1)S(1)}, bf16[48,1152]{1,0:T(8,128)(2,1)S(1)}, u32[]{:S(2)}, u32[]{:S(2)}) collective-permute-start(bf16[48,1152]{1,0:T(8,128)(2,1)S(1)} %get-tuple-element.73), channel_id=1, source_target_pairs={{0,12},{4,8},{8,4},{12,0},{16,28},{20,24},{24,20},{28,16},{32,44},... | collective-permute-start | bytes 331784 | tf_op jit(solution)/shard_map/ppermute | solution.py:24
  109.9 2.0 %collective-permute-done.13 = bf16[48,1152]{1,0:T(8,128)(2,1)S(1)} collective-permute-done((bf16[48,1152]{1,0:T(8,128)(2,1)S(1)}, bf16[48,1152]{1,0:T(8,128)(2,1)S(1)}, u32[]{:S(2)}, u32[]{:S(2)}) %collective-permute-start.13) | collective-permute-done | bytes 110624 | tf_op jit(solution)/shard_map/ppermute | solution.py:24
  124.1 2.1 %collective-permute-start.18 = (bf16[96,512]{1,0:T(8,128)(2,1)S(1)}, bf16[96,512]{1,0:T(8,128)(2,1)S(1)}, u32[]{:S(2)}, u32[]{:S(2)}) collective-permute-start(bf16[96,512]{1,0:T(8,128)(2,1)S(1)} %slice.81), channel_id=1, source_target_pairs={{0,12},{4,8},{8,4},{12,0},{16,28},{20,24},{24,20},{28,16},{32,44},... | collective-permute-start | bytes 294920 | tf_op jit(solution)/shard_map/ppermute | solution.py:24
  132.8 3.0 %collective-permute-start.24 = (bf16[96,512]{1,0:T(8,128)(2,1)S(1)}, bf16[96,512]{1,0:T(8,128)(2,1)S(1)}, u32[]{:S(2)}, u32[]{:S(2)}) collective-permute-start(bf16[96,512]{1,0:T(8,128)(2,1)S(1)} %slice.83), channel_id=1, source_target_pairs={{0,96},{4,100},{8,104},{12,108},{16,112},{20,116},{24,120},{28,124... | collective-permute-start | bytes 294920 | tf_op jit(solution)/shard_map/ppermute | solution.py:24
  136.3 2.5 %collective-permute-done.24.b3 = bf16[96,512]{1,0:T(8,128)(2,1)S(1)} collective-permute-done((bf16[96,512]{1,0:T(8,128)(2,1)S(1)}, bf16[96,512]{1,0:T(8,128)(2,1)S(1)}, u32[]{:S(2)}, u32[]{:S(2)}) %collective-permute-start.24) | collective-permute-done | bytes 98336 | tf_op jit(solution)/shard_map/ppermute | solution.py:24
  149.1 2.9 %collective-permute-done.28.r1_ref = bf16[256,384]{1,0:T(8,128)(2,1)S(1)} collective-permute-done((bf16[256,384]{1,0:T(8,128)(2,1)S(1)}, bf16[256,384]{1,0:T(8,128)(2,1)S(1)}, u32[]{:S(2)}, u32[]{:S(2)}) %collective-permute-start.28) | collective-permute-done | bytes 196640 | tf_op jit(solution)/shard_map/ppermute | solution.py:24
  (131 shorter events, 59.3 us)
Async XLA Ops:
  2.7 27.8 %collective-permute-start = (bf16[256,768]{1,0:T(8,128)(2,1)}, bf16[256,768]{1,0:T(8,128)(2,1)}, u32[]{:S(2)}, u32[]{:S(2)}) collective-permute-start(bf16[256,768]{1,0:T(8,128)(2,1)} %get-tuple-element.81), channel_id=1, source_target_pairs={{0,4},{4,0},{8,12},{12,8},{16,20},{20,16},{24,28},{28,24},{32,36},... | collective-permute-start | bytes 1179656 | tf_op jit(solution)/shard_map/ppermute | solution.py:24
  15.7 10.9 %collective-permute-start.1 = (bf16[256,768]{1,0:T(8,128)(2,1)}, bf16[256,768]{1,0:T(8,128)(2,1)}, u32[]{:S(2)}, u32[]{:S(2)}) collective-permute-start(bf16[256,768]{1,0:T(8,128)(2,1)} %get-tuple-element.48), channel_id=1, source_target_pairs={{0,4},{4,0},{8,12},{12,8},{16,20},{20,16},{24,28},{28,24},{32,36},... | collective-permute-start | bytes 1179656 | tf_op jit(solution)/shard_map/ppermute | solution.py:24
  72.0 7.8 %collective-permute-start.3 = (bf16[192,640]{1,0:T(8,128)(2,1)S(1)}, bf16[192,640]{1,0:T(8,128)(2,1)S(1)}, u32[]{:S(2)}, u32[]{:S(2)}) collective-permute-start(bf16[192,640]{1,0:T(8,128)(2,1)S(1)} %get-tuple-element.60), channel_id=1, source_target_pairs={{0,12},{4,8},{8,4},{12,0},{16,28},{20,24},{24,20},{28,16},{32,44},... | collective-permute-start | bytes 737288 | tf_op jit(solution)/shard_map/ppermute | solution.py:24
  74.6 9.6 %collective-permute-start.2 = (bf16[256,768]{1,0:T(8,128)(2,1)S(1)}, bf16[256,768]{1,0:T(8,128)(2,1)S(1)}, u32[]{:S(2)}, u32[]{:S(2)}) collective-permute-start(bf16[256,768]{1,0:T(8,128)(2,1)S(1)} %copy-done.10), channel_id=1, source_target_pairs={{0,4},{4,0},{8,12},{12,8},{16,20},{20,16},{24,28},{28,24},{32,36},... | collective-permute-start | bytes 1179656 | tf_op jit(solution)/shard_map/ppermute | solution.py:24
  75.6 15.6 %collective-permute-start.4 = (bf16[192,512]{1,0:T(8,128)(2,1)S(1)}, bf16[192,512]{1,0:T(8,128)(2,1)S(1)}, u32[]{:S(2)}, u32[]{:S(2)}) collective-permute-start(bf16[192,512]{1,0:T(8,128)(2,1)S(1)} %get-tuple-element.61), channel_id=1, source_target_pairs={{0,16},{4,20},{8,24},{12,28},{16,0},{20,4},{24,8},{28,12},{32,48},... | collective-permute-start | bytes 589832 | tf_op jit(solution)/shard_map/ppermute | solution.py:24
  79.8 17.3 %collective-permute-start.5 = (bf16[96,640]{1,0:T(8,128)(2,1)S(1)}, bf16[96,640]{1,0:T(8,128)(2,1)S(1)}, u32[]{:S(2)}, u32[]{:S(2)}) collective-permute-start(bf16[96,640]{1,0:T(8,128)(2,1)S(1)} %add_convert_fusion.1), channel_id=1, source_target_pairs={{0,16},{4,20},{8,24},{12,28},{16,0},{20,4},{24,8},{28,12},{32,48},... | collective-permute-start | bytes 368648 | tf_op jit(solution)/shard_map/ppermute | solution.py:24
  89.5 8.2 %collective-permute-start.10 = (bf16[192,512]{1,0:T(8,128)(2,1)S(1)}, bf16[192,512]{1,0:T(8,128)(2,1)S(1)}, u32[]{:S(2)}, u32[]{:S(2)}) collective-permute-start(bf16[192,512]{1,0:T(8,128)(2,1)S(1)} %get-tuple-element.69), channel_id=1, source_target_pairs={{0,32},{4,36},{8,40},{12,44},{16,48},{20,52},{24,56},{28,60},{32,0... | collective-permute-start | bytes 589832 | tf_op jit(solution)/shard_map/ppermute | solution.py:24
  91.2 5.9 %collective-permute-start.6 = (bf16[96,512]{1,0:T(8,128)(2,1)S(1)}, bf16[96,512]{1,0:T(8,128)(2,1)S(1)}, u32[]{:S(2)}, u32[]{:S(2)}) collective-permute-start(bf16[96,512]{1,0:T(8,128)(2,1)S(1)} %add_convert_fusion.3), channel_id=1, source_target_pairs={{0,12},{4,8},{8,4},{12,0},{16,28},{20,24},{24,20},{28,16},{32,44},... | collective-permute-start | bytes 294920 | tf_op jit(solution)/shard_map/ppermute | solution.py:24
  91.7 9.1 %collective-permute-start.9 = (bf16[192,640]{1,0:T(8,128)(2,1)S(1)}, bf16[192,640]{1,0:T(8,128)(2,1)S(1)}, u32[]{:S(2)}, u32[]{:S(2)}) collective-permute-start(bf16[192,640]{1,0:T(8,128)(2,1)S(1)} %get-tuple-element.68), channel_id=1, source_target_pairs={{0,96},{4,100},{8,104},{12,108},{16,112},{20,116},{24,120},{28,124... | collective-permute-start | bytes 737288 | tf_op jit(solution)/shard_map/ppermute | solution.py:24
  97.2 10.9 %collective-permute-start.7 = (bf16[48,1152]{1,0:T(8,128)(2,1)S(1)}, bf16[48,1152]{1,0:T(8,128)(2,1)S(1)}, u32[]{:S(2)}, u32[]{:S(2)}) collective-permute-start(bf16[48,1152]{1,0:T(8,128)(2,1)S(1)} %get-tuple-element.65), channel_id=1, source_target_pairs={{0,32},{4,36},{8,40},{12,44},{16,48},{20,52},{24,56},{28,60},{32,0... | collective-permute-start | bytes 331784 | tf_op jit(solution)/shard_map/ppermute | solution.py:24
  97.7 5.9 %collective-permute-start.12 = (bf16[96,512]{1,0:T(8,128)(2,1)S(1)}, bf16[96,512]{1,0:T(8,128)(2,1)S(1)}, u32[]{:S(2)}, u32[]{:S(2)}) collective-permute-start(bf16[96,512]{1,0:T(8,128)(2,1)S(1)} %add_convert_fusion.2), channel_id=1, source_target_pairs={{0,96},{4,100},{8,104},{12,108},{16,112},{20,116},{24,120},{28,124... | collective-permute-start | bytes 294920 | tf_op jit(solution)/shard_map/ppermute | solution.py:24
  105.9 6.0 %collective-permute-start.13 = (bf16[48,1152]{1,0:T(8,128)(2,1)S(1)}, bf16[48,1152]{1,0:T(8,128)(2,1)S(1)}, u32[]{:S(2)}, u32[]{:S(2)}) collective-permute-start(bf16[48,1152]{1,0:T(8,128)(2,1)S(1)} %get-tuple-element.73), channel_id=1, source_target_pairs={{0,12},{4,8},{8,4},{12,0},{16,28},{20,24},{24,20},{28,16},{32,44},... | collective-permute-start | bytes 331784 | tf_op jit(solution)/shard_map/ppermute | solution.py:24
  108.2 5.4 %collective-permute-start.8 = (bf16[24,1152]{1,0:T(8,128)(2,1)S(1)}, bf16[24,1152]{1,0:T(8,128)(2,1)S(1)}, u32[]{:S(2)}, u32[]{:S(2)}) collective-permute-start(bf16[24,1152]{1,0:T(8,128)(2,1)S(1)} %slice.93), channel_id=1, source_target_pairs={{0,96},{4,100},{8,104},{12,108},{16,112},{20,116},{24,120},{28,124... | collective-permute-start | bytes 165896 | tf_op jit(solution)/shard_map/ppermute | solution.py:24
  113.8 5.4 %collective-permute-start.15 = (bf16[24,1152]{1,0:T(8,128)(2,1)S(1)}, bf16[24,1152]{1,0:T(8,128)(2,1)S(1)}, u32[]{:S(2)}, u32[]{:S(2)}) collective-permute-start(bf16[24,1152]{1,0:T(8,128)(2,1)S(1)} %rescale.2), channel_id=1, source_target_pairs={{0,96},{4,100},{8,104},{12,108},{16,112},{20,116},{24,120},{28,124... | collective-permute-start | bytes 165896 | tf_op jit(solution)/shard_map/ppermute | solution.py:24
  121.1 7.5 %collective-permute-start.22 = (bf16[48,1152]{1,0:T(8,128)(2,1)S(1)}, bf16[48,1152]{1,0:T(8,128)(2,1)S(1)}, u32[]{:S(2)}, u32[]{:S(2)}) collective-permute-start(bf16[48,1152]{1,0:T(8,128)(2,1)S(1)} %pad_maximum_fusion.8), channel_id=1, source_target_pairs={{0,12},{4,8},{8,4},{12,0},{16,28},{20,24},{24,20},{28,16},{32,44},... | collective-permute-start | bytes 331784 | tf_op jit(solution)/shard_map/ppermute | solution.py:24
  124.1 5.9 %collective-permute-start.18 = (bf16[96,512]{1,0:T(8,128)(2,1)S(1)}, bf16[96,512]{1,0:T(8,128)(2,1)S(1)}, u32[]{:S(2)}, u32[]{:S(2)}) collective-permute-start(bf16[96,512]{1,0:T(8,128)(2,1)S(1)} %slice.81), channel_id=1, source_target_pairs={{0,12},{4,8},{8,4},{12,0},{16,28},{20,24},{24,20},{28,16},{32,44},... | collective-permute-start | bytes 294920 | tf_op jit(solution)/shard_map/ppermute | solution.py:24
  128.7 7.2 %collective-permute-start.23 = (bf16[96,640]{1,0:T(8,128)(2,1)S(1)}, bf16[96,640]{1,0:T(8,128)(2,1)S(1)}, u32[]{:S(2)}, u32[]{:S(2)}) collective-permute-start(bf16[96,640]{1,0:T(8,128)(2,1)S(1)} %slice.82), channel_id=1, source_target_pairs={{0,32},{4,36},{8,40},{12,44},{16,48},{20,52},{24,56},{28,60},{32,0... | collective-permute-start | bytes 368648 | tf_op jit(solution)/shard_map/ppermute | solution.py:24
  130.0 11.6 %collective-permute-start.20 = (bf16[192,512]{1,0:T(8,128)(2,1)S(1)}, bf16[192,512]{1,0:T(8,128)(2,1)S(1)}, u32[]{:S(2)}, u32[]{:S(2)}) collective-permute-start(bf16[192,512]{1,0:T(8,128)(2,1)S(1)} %pad_maximum_fusion.4), channel_id=1, source_target_pairs={{0,16},{4,20},{8,24},{12,28},{16,0},{20,4},{24,8},{28,12},{32,48},... | collective-permute-start | bytes 589832 | tf_op jit(solution)/shard_map/ppermute | solution.py:24
  131.6 10.0 %collective-permute-start.19 = (bf16[192,640]{1,0:T(8,128)(2,1)S(1)}, bf16[192,640]{1,0:T(8,128)(2,1)S(1)}, u32[]{:S(2)}, u32[]{:S(2)}) collective-permute-start(bf16[192,640]{1,0:T(8,128)(2,1)S(1)} %pad_maximum_fusion), channel_id=1, source_target_pairs={{0,12},{4,8},{8,4},{12,0},{16,28},{20,24},{24,20},{28,16},{32,44},... | collective-permute-start | bytes 737288 | tf_op jit(solution)/shard_map/ppermute | solution.py:24
  132.8 5.9 %collective-permute-start.24 = (bf16[96,512]{1,0:T(8,128)(2,1)S(1)}, bf16[96,512]{1,0:T(8,128)(2,1)S(1)}, u32[]{:S(2)}, u32[]{:S(2)}) collective-permute-start(bf16[96,512]{1,0:T(8,128)(2,1)S(1)} %slice.83), channel_id=1, source_target_pairs={{0,96},{4,100},{8,104},{12,108},{16,112},{20,116},{24,120},{28,124... | collective-permute-start | bytes 294920 | tf_op jit(solution)/shard_map/ppermute | solution.py:24
  135.9 8.6 %collective-permute-start.25 = (bf16[192,640]{1,0:T(8,128)(2,1)S(1)}, bf16[192,640]{1,0:T(8,128)(2,1)S(1)}, u32[]{:S(2)}, u32[]{:S(2)}) collective-permute-start(bf16[192,640]{1,0:T(8,128)(2,1)S(1)} %pad_maximum_fusion.1), channel_id=1, source_target_pairs={{0,96},{4,100},{8,104},{12,108},{16,112},{20,116},{24,120},{28,124... | collective-permute-start | bytes 737288 | tf_op jit(solution)/shard_map/ppermute | solution.py:24
  138.8 5.7 %collective-permute-start.26 = (bf16[192,512]{1,0:T(8,128)(2,1)S(1)}, bf16[192,512]{1,0:T(8,128)(2,1)S(1)}, u32[]{:S(2)}, u32[]{:S(2)}) collective-permute-start(bf16[192,512]{1,0:T(8,128)(2,1)S(1)} %pad_maximum_fusion.5), channel_id=1, source_target_pairs={{0,32},{4,36},{8,40},{12,44},{16,48},{20,52},{24,56},{28,60},{32,0... | collective-permute-start | bytes 589832 | tf_op jit(solution)/shard_map/ppermute | solution.py:24
  143.3 5.8 %collective-permute-start.27 = (bf16[256,384]{1,0:T(8,128)(2,1)S(1)}, bf16[256,384]{1,0:T(8,128)(2,1)S(1)}, u32[]{:S(2)}, u32[]{:S(2)}) collective-permute-start(bf16[256,384]{1,0:T(8,128)(2,1)S(1)} %get-tuple-element.77), channel_id=1, source_target_pairs={{0,4},{4,0},{8,12},{12,8},{16,20},{20,16},{24,28},{28,24},{32,36},... | collective-permute-start | bytes 589832 | tf_op jit(solution)/shard_map/ppermute | solution.py:24
  146.2 5.8 %collective-permute-start.28 = (bf16[256,384]{1,0:T(8,128)(2,1)S(1)}, bf16[256,384]{1,0:T(8,128)(2,1)S(1)}, u32[]{:S(2)}, u32[]{:S(2)}) collective-permute-start(bf16[256,384]{1,0:T(8,128)(2,1)S(1)} %get-tuple-element.78), channel_id=1, source_target_pairs={{0,4},{4,0},{8,12},{12,8},{16,20},{20,16},{24,28},{28,24},{32,36},... | collective-permute-start | bytes 589832 | tf_op jit(solution)/shard_map/ppermute | solution.py:24
  (24 other events, 161.8 us)
